TPU v7x, 32 devices: a whole 2x2x4 slice. The times are simulated.
32 devices in a mesh: exp: 4 (over z), tile: 8 (over y, x, core).
Axes of the slice: x: 2, y: 2, z: 4, core: 2. Of those that a mesh axis runs over, the one named last changes fastest.
Arguments:
- exposure: bfloat16 [4, 2048, 4096], P('exp', 'tile'), may hold values from -6 to 6
- row_taps: bfloat16 [3, 21], replicated, may hold values from -1.25 to 1.25
- column_taps: bfloat16 [3, 21], replicated, may hold values from -1.25 to 1.25
- basis_coef: float32 [4, 3], P('exp'), may hold values from -2.5 to 2.5
- warp_rows: bfloat16 [64, 128, 128], replicated, may hold values from -0.3 to 1.2
- warp_columns: bfloat16 [64, 128, 128], replicated, may hold values from -0.3 to 1.2
- warp_id: int32 [4, 8, 64], replicated, may hold values from 0 to 63
- route_device: int32 [4, 8, 64], replicated, may hold values from 0 to 31, as said below
- route_slot: int32 [4, 8, 64], replicated, may hold values from 0 to 63
- weight: float32 [4, 8], replicated, may hold values from 0.3 to 3
Outputs:
- coadd_patch: float32 [4096, 8192], P('exp', 'tile')
- difference: float32 [4, 2048, 4096], P('exp', 'tile')
Inputs may be any that keep to these rules, and one draw needn't show every extreme that they name: `route_device`: the blocks of one device (its exposures of its tile, in order) name any one device at most 4 times, and some device is named exactly 4 times by the blocks of every device.
All inputs are finite; a program needn't handle non-finite values.
Results may differ from a plain program's by a relative error of at most 0.0058.
Values may be sent and summed in bfloat16 or wider, within the bound.
A program may use at most 128 MiB of HBM per device.

v0:
```python
import jax
import jax.numpy as jnp
from jax import lax
from jax.sharding import PartitionSpec as P

BLOCK = 128
HALF = 10
SLOT_ROWS = 8
SLOT_COLS = 8


def extended(block, sides, width):
    for axis, dim in sides:
        count = lax.axis_size(axis)
        forward = [(i, i + 1) for i in range(count - 1)]
        backward = [(target, source) for source, target in forward]
        low = lax.ppermute(
            lax.slice_in_dim(block, block.shape[dim] - width, None, axis=dim), axis, forward
        )
        high = lax.ppermute(lax.slice_in_dim(block, 0, width, axis=dim), axis, backward)
        block = jnp.concatenate([low, block, high], axis=dim)
    return block


def band_matrices(tap_values, span_width, start_offset):
    offsets_grid = (
        lax.broadcasted_iota(jnp.int32, (BLOCK, span_width), 1)
        - lax.broadcasted_iota(jnp.int32, (BLOCK, span_width), 0)
        - start_offset
    )
    tap_index = jnp.arange(tap_values.shape[1], dtype=jnp.int32)
    tap_hits = (offsets_grid[None, :, :] == tap_index[:, None, None]).astype(jnp.float32)
    band_stack = jnp.einsum(
        "bj,jrc->brc", tap_values.astype(jnp.float32), tap_hits, precision=lax.Precision.HIGHEST
    )
    return band_stack.astype(jnp.bfloat16)


def kernel_match(padded, row_bands, column_bands, coef_row):
    tile_rows = padded.shape[0] - 2 * HALF
    tile_width = padded.shape[1]
    row_blocks = tile_rows // BLOCK
    col_blocks = tile_width // BLOCK
    top_rim = padded[:tile_rows].reshape(row_blocks, BLOCK, tile_width)[:, :HALF]
    centre = padded[HALF : HALF + tile_rows].reshape(row_blocks, BLOCK, tile_width)
    bottom_rim = padded[2 * HALF : 2 * HALF + tile_rows].reshape(row_blocks, BLOCK, tile_width)[
        :, BLOCK - HALF :
    ]
    windows = jnp.concatenate([top_rim, centre, bottom_rim], axis=1)
    summed = jnp.zeros((tile_rows, col_blocks, BLOCK), jnp.float32)
    for basis_idx in range(row_bands.shape[0]):
        row_pass = jnp.einsum(
            "ic,ncw->niw", row_bands[basis_idx], windows, preferred_element_type=jnp.float32
        )
        row_pass = (
            (coef_row[basis_idx] * row_pass)
            .astype(jnp.bfloat16)
            .reshape(tile_rows, col_blocks, BLOCK)
        )
        before = jnp.pad(row_pass, ((0, 0), (1, 0), (0, 0)))[:, :col_blocks]
        follow = jnp.pad(row_pass, ((0, 0), (0, 1), (0, 0)))[:, 1:]
        band_cols = column_bands[basis_idx]
        summed = summed + jnp.einsum(
            "rkj,ij->rki", before, band_cols[:, :BLOCK], preferred_element_type=jnp.float32
        )
        summed = summed + jnp.einsum(
            "rkj,ij->rki",
            row_pass,
            band_cols[:, BLOCK : 2 * BLOCK],
            preferred_element_type=jnp.float32,
        )
        summed = summed + jnp.einsum(
            "rkj,ij->rki", follow, band_cols[:, 2 * BLOCK :], preferred_element_type=jnp.float32
        )
    return summed.reshape(tile_rows, tile_width)


def shards(
    exposure,
    row_taps,
    column_taps,
    basis_coef,
    warp_rows,
    warp_columns,
    warp_id,
    route_device,
    route_slot,
    weight,
):
    n_exp = lax.axis_size("exp")
    n_tile = lax.axis_size("tile")
    devices = n_exp * n_tile
    exp_dev = exposure.shape[0]
    tile_rows = exposure.shape[1]
    tile_width = exposure.shape[2]
    row_blocks = tile_rows // BLOCK
    col_blocks = tile_width // BLOCK
    per_tile = row_blocks * col_blocks
    per_device = exp_dev * per_tile
    capacity = max(2, (2 * per_device + devices - 1) // devices)
    slot_count = SLOT_ROWS * SLOT_COLS
    pixels = BLOCK * BLOCK
    buffer_slots = devices * capacity
    myself = lax.axis_index("exp") * n_tile + lax.axis_index("tile")
    row_bands = band_matrices(row_taps, BLOCK + 2 * HALF, 0)
    column_bands = band_matrices(column_taps, 3 * BLOCK, BLOCK - HALF)

    def by_sender(source_table):
        shaped = source_table.reshape(n_exp, exp_dev, n_tile, per_tile).transpose(0, 2, 1, 3)
        return shaped.reshape(devices, per_device)

    padded = extended(exposure, (("tile", 1),), HALF)
    matched = jnp.stack([kernel_match(padded[0], row_bands, column_bands, basis_coef[0])]).astype(
        jnp.bfloat16
    )
    shaped = matched.reshape(exp_dev, row_blocks, BLOCK, col_blocks, BLOCK).transpose(0, 1, 3, 2, 4)
    my_blocks = shaped.reshape(per_device, BLOCK, BLOCK)
    dest_all = by_sender(route_device)
    slot_all = by_sender(route_slot)
    ident_all = by_sender(warp_id)
    weight_all = jnp.repeat(
        weight.reshape(n_exp, exp_dev, n_tile).transpose(0, 2, 1).reshape(devices, exp_dev),
        per_tile,
        axis=1,
    )
    earlier = jnp.arange(per_device)[:, None] > jnp.arange(per_device)[None, :]
    same_dest = dest_all[:, :, None] == dest_all[:, None, :]
    rank_all = jnp.sum(same_dest & earlier[None, :, :], axis=2)
    my_dest = lax.dynamic_index_in_dim(dest_all, myself, 0, keepdims=False)
    my_rank = lax.dynamic_index_in_dim(rank_all, myself, 0, keepdims=False)
    my_ident = lax.dynamic_index_in_dim(ident_all, myself, 0, keepdims=False)
    my_weight = lax.dynamic_index_in_dim(weight_all, myself, 0, keepdims=False)
    position = my_dest * capacity + my_rank
    pack_match = jnp.arange(buffer_slots, dtype=jnp.int32)[:, None] == position[None, :]
    pack_source = jnp.sum(
        jnp.where(pack_match, jnp.arange(per_device, dtype=jnp.int32)[None, :], 0), axis=1
    )
    pack_valid = jnp.any(pack_match, axis=1)
    recv_match = (dest_all[:, None, :] == myself) & (
        rank_all[:, None, :] == jnp.arange(capacity, dtype=jnp.int32)[None, :, None]
    )
    recv_slot = jnp.sum(jnp.where(recv_match, slot_all[:, None, :], 0), axis=2).reshape(
        buffer_slots
    )
    recv_weight = jnp.sum(jnp.where(recv_match, weight_all[:, None, :], 0.0), axis=2).reshape(
        buffer_slots
    )
    recv_valid = jnp.any(recv_match, axis=2).reshape(buffer_slots)
    slot_hot = (
        jnp.arange(slot_count, dtype=jnp.int32)[:, None] == recv_slot[None, :]
    ) & recv_valid[None, :]
    row_warp = warp_rows[my_ident]
    col_warp = warp_columns[my_ident]
    first_pass = jnp.einsum(
        "bij,bjc->bic", row_warp, my_blocks, preferred_element_type=jnp.float32
    ).astype(jnp.bfloat16)
    second_pass = jnp.einsum(
        "bic,bkc->bik", first_pass, col_warp, preferred_element_type=jnp.float32
    )
    weighted_mine = (my_weight[:, None, None] * second_pass).astype(jnp.bfloat16)
    packed = jnp.where(
        pack_valid[:, None, None], weighted_mine[pack_source], jnp.zeros((), jnp.bfloat16)
    )
    shaped = packed.reshape(devices, capacity, BLOCK, BLOCK)
    arrived = lax.all_to_all(shaped, ("exp", "tile"), split_axis=0, concat_axis=0, tiled=True)
    weighted = arrived.reshape(buffer_slots, BLOCK, BLOCK)
    slot_onehot = slot_hot.astype(jnp.bfloat16)
    numerator = jnp.dot(
        slot_onehot, weighted.reshape(buffer_slots, pixels), preferred_element_type=jnp.float32
    )
    denominator = jnp.dot(
        slot_hot.astype(jnp.float32), recv_weight, precision=lax.Precision.HIGHEST
    )
    coadd_slots = numerator / jnp.maximum(denominator, 1.0)[:, None]
    coadd_patch = (
        coadd_slots.reshape(SLOT_ROWS, SLOT_COLS, BLOCK, BLOCK)
        .transpose(0, 2, 1, 3)
        .reshape(SLOT_ROWS * BLOCK, SLOT_COLS * BLOCK)
    )
    picked = jnp.dot(
        slot_onehot.T, coadd_slots.astype(jnp.bfloat16), preferred_element_type=jnp.float32
    )
    picked = picked.astype(jnp.bfloat16).reshape(buffer_slots, BLOCK, BLOCK)
    shaped = picked.reshape(devices, capacity, BLOCK, BLOCK)
    arrived = lax.all_to_all(shaped, ("exp", "tile"), split_axis=0, concat_axis=0, tiled=True)
    returned = arrived.reshape(buffer_slots, BLOCK, BLOCK)
    row_warp = warp_rows[my_ident]
    col_warp = warp_columns[my_ident]
    first_pass = jnp.einsum(
        "bji,bjc->bic", row_warp, returned[position], preferred_element_type=jnp.float32
    ).astype(jnp.bfloat16)
    templates = jnp.einsum(
        "bic,bck->bik", first_pass, col_warp, preferred_element_type=jnp.float32
    ).astype(jnp.bfloat16)
    shaped = templates.reshape(exp_dev, row_blocks, col_blocks, BLOCK, BLOCK).transpose(
        0, 1, 3, 2, 4
    )
    template_image = shaped.reshape(exp_dev, tile_rows, tile_width)
    template_padded = extended(template_image, (("tile", 1),), HALF)
    difference = jnp.stack(
        [
            exposure[0].astype(jnp.float32)
            - kernel_match(template_padded[0], row_bands, column_bands, basis_coef[0])
        ]
    )
    return (coadd_patch, difference)


def solution(mesh):
    placed = (P("exp", "tile", None), P(), P(), P("exp", None), P(), P(), P(), P(), P(), P())
    return jax.shard_map(
        shards,
        mesh=mesh,
        in_specs=placed,
        out_specs=(P("exp", "tile"), P("exp", "tile", None)),
        check_vma=False,
    )
```

profile of v0, /device:TPU:1, one launch (start us, length us, event | category | flops | bytes accessed | tf_op | source)
XLA Modules:
  0.0 417.2 jit_solution(11544356337202096191)
XLA Ops:
  1.8 4.5 %collective-permute-start = (bf16[1,10,4096]{2,1,0:T(8,128)(2,1)S(1)}, bf16[1,10,4096]{2,1,0:T(8,128)(2,1)S(1)}, u32[]{:S(2)}, u32[]{:S(2)}) collective-permute-start(bf16[1,10,4096]{2,1,0:T(8,128)(2,1)S(1)} %get-tuple-element.10), channel_id=1, source_target_pairs={{0,1},{1,2},{2,3},{3,4},{4,5},{5,6},{6,7},{8,9},{9,10},{10,11},{11... | collective-permute-start | bytes 245768 | tf_op jit(solution)/shard_map/ppermute | solution.py:17
  19.3 3.9 gather_fusion.1
  28.6 4.2 %copy.49 = bf16[2,128,4096]{2,1,0:T(8,128)(2,1)} copy(bf16[2,128,4096]{1,2,0:T(8,128)(2,1)} %fusion.10) | data formatting | bytes 4194304 | tf_op jit(solution)/shard_map/convert_element_type | solution.py:57
  34.9 3.7 fusion.51
  61.4 4.3 %copy.45 = bf16[2,128,4096]{2,1,0:T(8,128)(2,1)} copy(bf16[2,128,4096]{1,2,0:T(8,128)(2,1)} %fusion.11) | data formatting | bytes 4194304 | tf_op jit(solution)/shard_map/convert_element_type | solution.py:57
  67.8 3.7 fusion.57
  77.8 10.0 %add_convert_fusion = bf16[256,32,128]{2,0,1:T(8,128)(2,1)S(1)} fusion(f32[256,32,128]{2,0,1:T(8,128)} %fusion.47, f32[256,32,128]{2,0,1:T(8,128)} %fusion.49, f32[256,32,128]{2,0,1:T(8,128)S(1)} %copy-done.6, f32[256,32,128]{2,0,1:T(8,128)S(1)} %copy-done.7, f32[256,32,128]{2,0,1:T(8,128)} %fusion.55, f32[256,32,128]{2,0,1:T(8,128)} %fusion.57, ...), kind=kOutput, calls=%fused_computation.32 | convolution fusion | flops 269484032 | bytes 37781504 | tf_op jit(solution)/shard_map/rkj,ij->rki/dot_general | solution.py:72
  89.3 5.6 %multiply_convert_fusion = bf16[64,128,128]{2,1,0:T(8,128)(2,1)S(1)} fusion(bf16[64,128,128]{2,1,0:T(8,128)(2,1)} %gather_fusion.1, bf16[64,128,128]{2,1,0:T(8,128)(2,1)} %gather_fusion, bf16[64,128,128]{2,1,0:T(8,128)(2,1)} %bitcast.203, f32[]{:T(128)} %bitcast.3), kind=kOutput, calls=%fused_computation.31 | convolution fusion | flops 540016640 | bytes 8388612 | tf_op jit(solution)/shard_map/bic,bkc->bik/dot_general | solution.py:157
  98.0 4.6 %broadcast_select_fusion = bf16[32,4,128,128]{3,2,1,0:T(8,128)(2,1)} fusion(bf16[32,4,128,128]{3,2,1,0:T(8,128)(2,1)} %bitcast.191, pred[32,4]{1,0:T(8,128)(4,1)S(1)} %broadcast_in_dim.78), kind=kLoop, calls=%fused_computation.33 | loop fusion | flops 2097152 | bytes 8388736 | tf_op jit(solution)/shard_map/jit(_where)/select_n | solution.py:161
  102.5 6.9 %all-to-all-start = ((bf16[32,4,128,128]{3,2,1,0:T(8,128)(2,1)}), bf16[32,4,128,128]{3,2,1,0:T(8,128)(2,1)}, u32[]{:S(2)}, u32[]{:S(2)}) async-start(bf16[32,4,128,128]{3,2,1,0:T(8,128)(2,1)} %broadcast_select_fusion), calls=%async_computation | async-start | bytes 8388608 | tf_op jit(solution)/shard_map/all_to_all | solution.py:165
  110.7 91.9 %all-to-all-done = bf16[32,4,128,128]{3,2,1,0:T(8,128)(2,1)} async-done(((bf16[32,4,128,128]{3,2,1,0:T(8,128)(2,1)}), bf16[32,4,128,128]{3,2,1,0:T(8,128)(2,1)}, u32[]{:S(2)}, u32[]{:S(2)}) %all-to-all-start) | async-done | bytes 4194336 | tf_op jit(solution)/shard_map/all_to_all | solution.py:165
  202.6 5.1 %convolution_divide_fusion = f32[64,16384]{1,0:T(8,128)S(1)} fusion(bf16[16,8,128,128]{3,2,1,0:T(8,128)(2,1)} %bitcast.67, f32[64]{0:T(128)S(1)} %fusion.67, s32[128]{0:T(128)S(1)} %eq.102, pred[128]{0:T(512)(128)(4,1)S(1)} %and.32), kind=kOutput, calls=%fused_computation.5 | convolution fusion | flops 269500416 | bytes 8389504 | tf_op jit(solution)/shard_map/dot_general | solution.py:168
  214.2 4.6 %all-to-all-start.1 = ((bf16[32,4,128,128]{3,2,1,0:T(8,128)(2,1)}), bf16[32,4,128,128]{3,2,1,0:T(8,128)(2,1)}, u32[]{:S(2)}, u32[]{:S(2)}) async-start(bf16[32,4,128,128]{3,2,1,0:T(8,128)(2,1)} %bitcast.190), calls=%async_computation.1 | async-start | bytes 8388608 | tf_op jit(solution)/shard_map/all_to_all | solution.py:185
  218.9 93.3 %all-to-all-done.1 = bf16[32,4,128,128]{3,2,1,0:T(8,128)(2,1)} async-done(((bf16[32,4,128,128]{3,2,1,0:T(8,128)(2,1)}), bf16[32,4,128,128]{3,2,1,0:T(8,128)(2,1)}, u32[]{:S(2)}, u32[]{:S(2)}) %all-to-all-start.1) | async-done | bytes 4194336 | tf_op jit(solution)/shard_map/all_to_all | solution.py:185
  312.2 4.3 %gather_fusion.3 = bf16[64,128,128]{2,1,0:T(8,128)(2,1)} fusion(bf16[128,128,128]{2,1,0:T(8,128)(2,1)} %bitcast.38, s32[1024]{0:T(1024)S(1)} %pad_clamp_fusion), kind=kCustom, calls=%fused_computation.3 | custom fusion | bytes 4194560 | tf_op jit(solution)/shard_map/gather | solution.py:190
  316.5 5.8 %fusion.25 = bf16[64,128,128]{1,2,0:T(8,128)(2,1)} fusion(bf16[64,128,128]{2,1,0:T(8,128)(2,1)} %gather_fusion.1, bf16[64,128,128]{2,1,0:T(8,128)(2,1)S(1)} %copy-done.2, bf16[64,128,128]{2,1,0:T(8,128)(2,1)} %gather_fusion.3), kind=kOutput, calls=%fused_computation.48 | convolution fusion | flops 538968064 | bytes 8388608 | tf_op jit(solution)/shard_map/bic,bck->bik/dot_general | solution.py:192
  322.3 3.4 copy.61
  329.1 3.7 collective-permute-start.2
  334.7 5.2 %copy.160 = f32[128,8,8,128]{3,1,2,0:T(8,128)} copy(f32[128,8,8,128]{3,2,1,0:T(8,128)} %bitcast.189) | data formatting | bytes 8388608
  359.0 4.1 fusion.40
  376.5 4.0 fusion.34
  393.5 12.0 %add_add_fusion = f32[256,32,128]{0,2,1:T(8,128)} fusion(f32[256,32,128]{0,2,1:T(8,128)} %fusion.30, f32[256,32,128]{0,2,1:T(8,128)} %fusion.32, f32[256,32,128]{0,2,1:T(8,128)} %fusion.34, f32[256,32,128]{0,2,1:T(8,128)} %fusion.36, f32[256,32,128]{0,2,1:T(8,128)} %fusion.38, f32[256,32,128]{0,2,1:T(8,128)} %fusion.40, f32[256,32,128]{0,2,1:T(8,128)S(1)} %copy-done.5, ...), kind=kOutput, calls=%fused_computation.29 | convolution fusion | flops 268435456 | bytes 39878656 | tf_op jit(solution)/shard_map/rkj,ij->rki/dot_general | solution.py:72
  405.6 5.6 %copy.74 = f32[1,256,4096]{2,1,0:T(8,128)} copy(f32[1,256,4096]{1,2,0:T(8,128)} %bitcast.192) | data formatting | bytes 8388608 | tf_op jit(solution)/shard_map/reshape | solution.py:75
  411.2 5.7 %convert_subtract_fusion = f32[1,256,4096]{2,1,0:T(8,128)} fusion(f32[1,256,4096]{2,1,0:T(8,128)} %copy.74, bf16[1,256,4096]{2,1,0:T(8,128)(2,1)} %param.10), kind=kLoop, calls=%fused_computation.30 | loop fusion | flops 2097152 | bytes 10485760 | tf_op jit(solution)/shard_map/sub | solution.py:202
  (120 shorter events, 115.8 us)
Async XLA Ops:
  0.6 16.5 %copy-start = (bf16[64,128,128]{2,1,0:T(8,128)(2,1)S(1)}, bf16[64,128,128]{2,1,0:T(8,128)(2,1)}, u32[]{:S(2)}) copy-start(bf16[64,128,128]{2,1,0:T(8,128)(2,1)} %param.14) | copy-start | bytes 6291460
  1.8 22.3 %collective-permute-start = (bf16[1,10,4096]{2,1,0:T(8,128)(2,1)S(1)}, bf16[1,10,4096]{2,1,0:T(8,128)(2,1)S(1)}, u32[]{:S(2)}, u32[]{:S(2)}) collective-permute-start(bf16[1,10,4096]{2,1,0:T(8,128)(2,1)S(1)} %get-tuple-element.10), channel_id=1, source_target_pairs={{0,1},{1,2},{2,3},{3,4},{4,5},{5,6},{6,7},{8,9},{9,10},{10,11},{11... | collective-permute-start | bytes 245768 | tf_op jit(solution)/shard_map/ppermute | solution.py:17
  6.3 17.8 %collective-permute-start.1 = (bf16[1,10,4096]{2,1,0:T(8,128)(2,1)S(1)}, bf16[1,10,4096]{2,1,0:T(8,128)(2,1)S(1)}, u32[]{:S(2)}, u32[]{:S(2)}) collective-permute-start(bf16[1,10,4096]{2,1,0:T(8,128)(2,1)S(1)} %get-tuple-element.11), channel_id=1, source_target_pairs={{1,0},{2,1},{3,2},{4,3},{5,4},{6,5},{7,6},{9,8},{10,9},{11,10},{12... | collective-permute-start | bytes 245768 | tf_op jit(solution)/shard_map/ppermute | solution.py:20
  19.3 3.9 copy-start.18
  19.3 4.8 %copy-start.8 = (bf16[1,256,4096]{2,1,0:T(8,128)(2,1)S(1)}, bf16[1,256,4096]{2,1,0:T(8,128)(2,1)}, u32[]{:S(2)}) copy-start(bf16[1,256,4096]{2,1,0:T(8,128)(2,1)} %param.10) | copy-start | bytes 6291460
  41.9 3.0 copy-start.9
  54.7 3.4 copy-start.10
  54.7 3.4 copy-start.15
  71.5 6.3 %copy-start.7 = (f32[256,32,128]{2,0,1:T(8,128)S(1)}, f32[256,32,128]{2,0,1:T(8,128)}, u32[]{:S(2)}) copy-start(f32[256,32,128]{2,0,1:T(8,128)} %fusion.53) | copy-start | bytes 12582916
  74.8 3.0 copy-start.6
  102.5 6.9 %copy-start.14 = (s32[4,8,64]{2,1,0:T(8,128)S(1)}, s32[4,8,64]{2,1,0:T(8,128)}, u32[]{:S(2)}) copy-start(s32[4,8,64]{2,1,0:T(8,128)} %param.17) | copy-start | bytes 24580
  102.5 6.9 %copy-start.17 = (s32[4,8,64]{2,1,0:T(8,128)S(1)}, s32[4,8,64]{2,1,0:T(8,128)}, u32[]{:S(2)}) copy-start(s32[4,8,64]{2,1,0:T(8,128)} %param.18) | copy-start | bytes 24580
  102.5 100.1 %all-to-all-start = ((bf16[32,4,128,128]{3,2,1,0:T(8,128)(2,1)}), bf16[32,4,128,128]{3,2,1,0:T(8,128)(2,1)}, u32[]{:S(2)}, u32[]{:S(2)}) async-start(bf16[32,4,128,128]{3,2,1,0:T(8,128)(2,1)} %broadcast_select_fusion), calls=%async_computation | async-start | bytes 8388608 | tf_op jit(solution)/shard_map/all_to_all | solution.py:165
  214.2 97.9 %all-to-all-start.1 = ((bf16[32,4,128,128]{3,2,1,0:T(8,128)(2,1)}), bf16[32,4,128,128]{3,2,1,0:T(8,128)(2,1)}, u32[]{:S(2)}, u32[]{:S(2)}) async-start(bf16[32,4,128,128]{3,2,1,0:T(8,128)(2,1)} %bitcast.190), calls=%async_computation.1 | async-start | bytes 8388608 | tf_op jit(solution)/shard_map/all_to_all | solution.py:185
  218.8 97.7 %copy-start.2 = (bf16[64,128,128]{2,1,0:T(8,128)(2,1)S(1)}, bf16[64,128,128]{2,1,0:T(8,128)(2,1)}, u32[]{:S(2)}) copy-start(bf16[64,128,128]{2,1,0:T(8,128)(2,1)} %gather_fusion) | copy-start | bytes 6291460
  329.1 13.2 %collective-permute-start.2 = (bf16[1,10,4096]{2,1,0:T(8,128)(2,1)S(1)}, bf16[1,10,4096]{2,1,0:T(8,128)(2,1)S(1)}, u32[]{:S(2)}, u32[]{:S(2)}) collective-permute-start(bf16[1,10,4096]{2,1,0:T(8,128)(2,1)S(1)} %get-tuple-element.6), channel_id=1, source_target_pairs={{0,1},{1,2},{2,3},{3,4},{4,5},{5,6},{6,7},{8,9},{9,10},{10,11},{11... | collective-permute-start | bytes 245768 | tf_op jit(solution)/shard_map/ppermute | solution.py:17
  332.8 9.6 %collective-permute-start.3 = (bf16[1,10,4096]{2,1,0:T(8,128)(2,1)S(1)}, bf16[1,10,4096]{2,1,0:T(8,128)(2,1)S(1)}, u32[]{:S(2)}, u32[]{:S(2)}) collective-permute-start(bf16[1,10,4096]{2,1,0:T(8,128)(2,1)S(1)} %get-tuple-element.7), channel_id=1, source_target_pairs={{1,0},{2,1},{3,2},{4,3},{5,4},{6,5},{7,6},{9,8},{10,9},{11,10},{12... | collective-permute-start | bytes 245768 | tf_op jit(solution)/shard_map/ppermute | solution.py:20
  342.4 3.5 copy-start.11
  342.4 3.5 copy-start.16
  359.0 4.1 copy-start.12
  376.5 4.0 copy-start.13
  387.2 6.3 %copy-start.5 = (f32[256,32,128]{0,2,1:T(8,128)S(1)}, f32[256,32,128]{0,2,1:T(8,128)}, u32[]{:S(2)}) copy-start(f32[256,32,128]{0,2,1:T(8,128)} %fusion.44) | copy-start | bytes 12582916
  390.2 3.4 copy-start.4
  411.2 5.7 %copy-start.1 = (bf16[64,128,128]{2,1,0:T(8,128)(2,1)S(1)}, bf16[64,128,128]{2,1,0:T(8,128)(2,1)}, u32[]{:S(2)}) copy-start(bf16[64,128,128]{2,1,0:T(8,128)(2,1)} %param.14) | copy-start | bytes 6291460
  (1 other events, 2.0 us)
where the time goes:
time: 423 us; the launch traced here: 417 us
  waiting for transfers between devices  185 us (44%)
  matrix products  111 us (26%)
  local copies, waits for them, and re-layouts  78.1 us (18%)
  starting transfers between devices  23.5 us (6%)
  other arithmetic  18.5 us (4%)
    all_to_all x2, waiting for transfers between devices, shards(): lax.all_to_all(shaped, ('exp', 'tile'), split_axis=0, concat_axis=0, tile...  185 us
    dot_general x6, matrix products, kernel_match(): jnp.einsum('rkj,ij->rki', follow, band_cols[:, 2 * BLOCK:], preferred_ele...  37.4 us
    unnamed x48, local copies, waits for them, and re-layouts  23 us
    dot_general x6, matrix products, kernel_match(): jnp.einsum('rkj,ij->rki', row_pass, band_cols[:, BLOCK:2 * BLOCK], prefer...  20 us
    convert_element_type x6, local copies, waits for them, and re-layouts, kernel_match(): row_pass = (coef_row[basis_idx] * row_pass).astype(jnp.bfloat16).reshape(...  19.9 us
    dot_general x6, matrix products, kernel_match(): jnp.einsum('rkj,ij->rki', before, band_cols[:, :BLOCK], preferred_element...  17.7 us
    dot_general x6, matrix products, kernel_match(): jnp.einsum('ic,ncw->niw', row_bands[basis_idx], windows, preferred_elemen...  14.7 us
    all_to_all x2, starting transfers between devices, shards(): lax.all_to_all(shaped, ('exp', 'tile'), split_axis=0, concat_axis=0, tile...  11.5 us
  transfers between devices with their start and end apart: 6, of which 2 were waited for; matrix products, arithmetic and copies ran while one was open for 6% of the time, Pallas kernels for 0%

commit v1 on v0

v1 whole, which is shorter than its diff:
```python
import functools

import jax
import jax.numpy as jnp
from jax import lax
from jax.experimental import pallas as pl
from jax.experimental.pallas import tpu as pltpu
from jax.sharding import PartitionSpec as P

BLOCK = 128
HALF = 10
RIM = 16
WIDE = 2 * BLOCK
SLOT_ROWS = 8
SLOT_COLS = 8
VMEM_BYTES = 56 * 1024 * 1024


def halo(image, axis):
    count = lax.axis_size(axis)
    forward = [(i, i + 1) for i in range(count - 1)]
    backward = [(target, source) for source, target in forward]
    above = lax.ppermute(image[-RIM:], axis, forward)
    below = lax.ppermute(image[:RIM], axis, backward)
    return above, below


def banded(taps, rows, cols, offset, transposed):
    shape = (rows, cols)
    lag = lax.broadcasted_iota(jnp.int32, shape, 1) - lax.broadcasted_iota(jnp.int32, shape, 0)
    lag = lag - offset
    if transposed:
        lag = lag.T
    count = taps.shape[1]
    hit = lag[None, :, :] == jnp.arange(count, dtype=jnp.int32)[:, None, None]
    picked = jnp.where(hit[None], taps[:, :, None, None], jnp.zeros((), taps.dtype))
    return jnp.sum(picked.astype(jnp.float32), axis=1).astype(jnp.bfloat16)


def row_stage(coef, above, image, below, row_bands, padded, passes):
    bases = passes.shape[0]
    rows, cols = image.shape
    blocks = rows // BLOCK
    span = BLOCK + 2 * RIM
    padded[:RIM, :] = above[...]
    padded[RIM : RIM + rows, :] = image[...]
    padded[RIM + rows :, :] = below[...]
    edge = jnp.zeros((rows, BLOCK), passes.dtype)
    for basis in range(bases):
        passes[basis, :, :BLOCK] = edge
        passes[basis, :, BLOCK + cols :] = edge

    def step(at, carry):
        start = pl.multiple_of(at * WIDE, WIDE)
        for block in range(blocks):
            top = block * BLOCK
            sums = jnp.dot(
                row_bands[...],
                padded[top : top + span, pl.ds(start, WIDE)],
                preferred_element_type=jnp.float32,
            )
            for basis in range(bases):
                scaled = coef[0, basis] * sums[basis * BLOCK : (basis + 1) * BLOCK]
                passes[basis, top : top + BLOCK, pl.ds(start + BLOCK, WIDE)] = scaled.astype(
                    passes.dtype
                )
        return carry

    lax.fori_loop(0, cols // WIDE, step, 0, unroll=2)


def column_chunk(passes, column_bands, start):
    total = None
    for basis in range(passes.shape[0]):
        term = jnp.dot(
            passes[basis, :, pl.ds(start, 2 * WIDE)],
            column_bands[basis],
            preferred_element_type=jnp.float32,
        )
        total = term if total is None else total + term
    return total


def forward_kernel(
    coef, ident, place, weight, above, image, below, row_bands, column_bands, warp_rows,
    warp_columns, packed, padded, passes,
):
    rows, cols = image.shape
    blocks = rows // BLOCK
    across = cols // BLOCK
    row_stage(coef, above, image, below, row_bands, padded, passes)
    blank = jnp.zeros((BLOCK, BLOCK), packed.dtype)

    def clear(at, carry):
        packed[at] = blank
        return carry

    lax.fori_loop(0, packed.shape[0], clear, 0, unroll=4)
    scale = weight[0]

    def step(at, carry):
        start = pl.multiple_of(at * WIDE, WIDE)
        matched = column_chunk(passes, column_bands, start).astype(jnp.bfloat16)
        for block in range(blocks):
            for side in range(WIDE // BLOCK):
                number = block * across + at * (WIDE // BLOCK) + side
                which = ident[number]
                piece = matched[
                    block * BLOCK : (block + 1) * BLOCK, side * BLOCK : (side + 1) * BLOCK
                ]
                first = jnp.dot(
                    warp_rows[which], piece, preferred_element_type=jnp.float32
                ).astype(jnp.bfloat16)
                second = lax.dot_general(
                    first,
                    warp_columns[which],
                    (((1,), (1,)), ((), ())),
                    preferred_element_type=jnp.float32,
                )
                packed[place[number]] = (scale * second).astype(packed.dtype)
        return carry

    lax.fori_loop(0, cols // WIDE, step, 0, unroll=2)


def coadd_kernel(slot, valid, inverse, arrived, patch, picked):
    side = SLOT_COLS * BLOCK
    blank = jnp.zeros((BLOCK, side), jnp.float32)
    for row in range(SLOT_ROWS):
        patch[row * BLOCK : (row + 1) * BLOCK, :] = blank

    def where(number):
        top = pl.multiple_of((number // SLOT_COLS) * BLOCK, BLOCK)
        left = pl.multiple_of((number % SLOT_COLS) * BLOCK, BLOCK)
        return pl.ds(top, BLOCK), pl.ds(left, BLOCK)

    def add(at, carry):
        @pl.when(valid[at] != 0)
        def _():
            spot = where(slot[at])
            patch[spot] = patch[spot] + arrived[at].astype(jnp.float32)

        return carry

    lax.fori_loop(0, arrived.shape[0], add, 0)

    def divide(at, carry):
        spot = where(at)
        patch[spot] = patch[spot] * inverse[at]
        return carry

    lax.fori_loop(0, SLOT_ROWS * SLOT_COLS, divide, 0, unroll=4)

    def pick(at, carry):
        picked[at] = patch[where(slot[at])].astype(picked.dtype)
        return carry

    lax.fori_loop(0, arrived.shape[0], pick, 0, unroll=4)


def unwarp_kernel(ident, place, returned, warp_rows, warp_columns, image):
    rows, cols = image.shape
    blocks = rows // BLOCK
    across = cols // BLOCK

    def step(at, carry):
        start = pl.multiple_of(at * WIDE, WIDE)
        for block in range(blocks):
            for side in range(WIDE // BLOCK):
                number = block * across + at * (WIDE // BLOCK) + side
                which = ident[number]
                back = lax.dot_general(
                    warp_rows[which],
                    returned[place[number]],
                    (((0,), (0,)), ((), ())),
                    preferred_element_type=jnp.float32,
                ).astype(jnp.bfloat16)
                piece = jnp.dot(back, warp_columns[which], preferred_element_type=jnp.float32)
                image[
                    block * BLOCK : (block + 1) * BLOCK, pl.ds(start + side * BLOCK, BLOCK)
                ] = piece.astype(image.dtype)
        return carry

    lax.fori_loop(0, cols // WIDE, step, 0, unroll=2)


def difference_kernel(
    coef, above, image, below, row_bands, column_bands, exposure, difference, padded, passes
):
    cols = image.shape[1]
    row_stage(coef, above, image, below, row_bands, padded, passes)

    def step(at, carry):
        start = pl.multiple_of(at * WIDE, WIDE)
        matched = column_chunk(passes, column_bands, start)
        spot = pl.ds(start, WIDE)
        difference[:, spot] = exposure[:, spot].astype(jnp.float32) - matched
        return carry

    lax.fori_loop(0, cols // WIDE, step, 0, unroll=2)


def scalars(count):
    return [pl.BlockSpec(memory_space=pltpu.SMEM)] * count


def vectors(count):
    return [pl.BlockSpec(memory_space=pltpu.VMEM)] * count


def shards(
    exposure, row_taps, column_taps, basis_coef, warp_rows, warp_columns, warp_id, route_device,
    route_slot, weight,
):
    n_exp = lax.axis_size("exp")
    n_tile = lax.axis_size("tile")
    devices = n_exp * n_tile
    rows, cols = exposure.shape[1:]
    bases = row_taps.shape[0]
    blocks = (rows // BLOCK) * (cols // BLOCK)
    capacity = max(2, (2 * blocks + devices - 1) // devices)
    slots = SLOT_ROWS * SLOT_COLS
    buffered = devices * capacity
    myself = lax.axis_index("exp") * n_tile + lax.axis_index("tile")
    params = pltpu.CompilerParams(vmem_limit_bytes=VMEM_BYTES)
    mine = exposure[0]

    above, below = halo(mine, "tile")
    row_bands = banded(row_taps, BLOCK, BLOCK + 2 * RIM, RIM - HALF, False)
    row_bands = row_bands.reshape(bases * BLOCK, BLOCK + 2 * RIM)
    column_bands = banded(column_taps, WIDE, 2 * WIDE, BLOCK - HALF, True)

    dest_all = route_device.reshape(devices, blocks)
    slot_all = route_slot.reshape(devices, blocks)
    weight_all = weight.reshape(devices)
    earlier = jnp.arange(blocks)[:, None] > jnp.arange(blocks)[None, :]
    same = dest_all[:, :, None] == dest_all[:, None, :]
    rank_all = jnp.sum(same & earlier[None], axis=2, dtype=jnp.int32)
    place_all = dest_all * capacity + rank_all
    place = lax.dynamic_index_in_dim(place_all, myself, 0, keepdims=False)
    ident = lax.dynamic_index_in_dim(warp_id.reshape(devices, blocks), myself, 0, keepdims=False)
    my_weight = lax.dynamic_index_in_dim(weight_all, myself, 0, keepdims=True)
    hit = (dest_all[:, None, :] == myself) & (
        rank_all[:, None, :] == jnp.arange(capacity, dtype=jnp.int32)[None, :, None]
    )
    slot = jnp.sum(jnp.where(hit, slot_all[:, None, :], 0), axis=2, dtype=jnp.int32)
    slot = slot.reshape(buffered)
    valid = jnp.any(hit, axis=2).reshape(buffered).astype(jnp.int32)
    owned = (slot_all[None] == jnp.arange(slots, dtype=jnp.int32)[:, None, None]) & (
        dest_all == myself
    )[None]
    total = jnp.sum(jnp.where(owned, weight_all[None, :, None], 0.0), axis=(1, 2))
    inverse = 1.0 / jnp.maximum(total, 1.0)

    work = [
        pltpu.VMEM((rows + 2 * RIM, cols), jnp.bfloat16),
        pltpu.VMEM((bases, rows, cols + 2 * BLOCK), jnp.bfloat16),
    ]
    packed = pl.pallas_call(
        forward_kernel,
        out_shape=jax.ShapeDtypeStruct((buffered, BLOCK, BLOCK), jnp.bfloat16),
        in_specs=scalars(4) + vectors(7),
        out_specs=pl.BlockSpec(memory_space=pltpu.VMEM),
        scratch_shapes=work,
        compiler_params=params,
    )(
        basis_coef, ident, place, my_weight, above, mine, below, row_bands, column_bands,
        warp_rows, warp_columns,
    )
    packed = packed.reshape(devices, capacity, BLOCK, BLOCK)
    arrived = lax.all_to_all(packed, ("exp", "tile"), split_axis=0, concat_axis=0, tiled=True)
    patch, picked = pl.pallas_call(
        coadd_kernel,
        out_shape=(
            jax.ShapeDtypeStruct((SLOT_ROWS * BLOCK, SLOT_COLS * BLOCK), jnp.float32),
            jax.ShapeDtypeStruct((buffered, BLOCK, BLOCK), jnp.bfloat16),
        ),
        in_specs=scalars(3) + vectors(1),
        out_specs=tuple(vectors(2)),
        compiler_params=params,
    )(slot, valid, inverse, arrived.reshape(buffered, BLOCK, BLOCK))
    picked = picked.reshape(devices, capacity, BLOCK, BLOCK)
    returned = lax.all_to_all(picked, ("exp", "tile"), split_axis=0, concat_axis=0, tiled=True)
    template = pl.pallas_call(
        unwarp_kernel,
        out_shape=jax.ShapeDtypeStruct((rows, cols), jnp.bfloat16),
        in_specs=scalars(2) + vectors(3),
        out_specs=pl.BlockSpec(memory_space=pltpu.VMEM),
        compiler_params=params,
    )(ident, place, returned.reshape(buffered, BLOCK, BLOCK), warp_rows, warp_columns)
    template_above, template_below = halo(template, "tile")
    difference = pl.pallas_call(
        difference_kernel,
        out_shape=jax.ShapeDtypeStruct((rows, cols), jnp.float32),
        in_specs=scalars(1) + vectors(6),
        out_specs=pl.BlockSpec(memory_space=pltpu.VMEM),
        scratch_shapes=work,
        compiler_params=params,
    )(
        basis_coef, template_above, template, template_below, row_bands, column_bands, mine
    )
    return patch, difference[None]


def solution(mesh):
    placed = (P("exp", "tile", None), P(), P(), P("exp", None), P(), P(), P(), P(), P(), P())
    return jax.shard_map(
        shards,
        mesh=mesh,
        in_specs=placed,
        out_specs=(P("exp", "tile"), P("exp", "tile", None)),
        check_vma=False,
    )
```

time: 423 us -> 287 us (0.68)
  the two profiles are of different devices: /device:TPU:1 before, /device:TPU:11 now
where the time goes in v1:
time: 287 us; the launch traced here: 286 us
  blocking collectives  100 us (35%)
  waiting for transfers between devices  89.8 us (31%)
  Pallas kernels  59.1 us (21%)
  starting transfers between devices  17.8 us (6%)
  other arithmetic  10.9 us (4%)
  local copies, waits for them, and re-layouts  6.86 us (2%)
    all_to_all x1, blocking collectives, shards(): lax.all_to_all(picked, ('exp', 'tile'), split_axis=0, concat_axis=0, tile...  100 us
    all_to_all x1, waiting for transfers between devices, shards(): lax.all_to_all(packed, ('exp', 'tile'), split_axis=0, concat_axis=0, tile...  87.9 us
    pallas_call x1, Pallas kernels, shards(): pl.pallas_call(forward_kernel, out_shape=jax.ShapeDtypeStruct((buffered,...  27.4 us
    pallas_call x1, Pallas kernels, shards(): pl.pallas_call(difference_kernel, out_shape=jax.ShapeDtypeStruct((rows, c...  12.6 us
    pallas_call x1, Pallas kernels, shards(): pl.pallas_call(coadd_kernel, out_shape=(jax.ShapeDtypeStruct((SLOT_ROWS *...  10.9 us
    ppermute x2, starting transfers between devices, halo(): above = lax.ppermute(image[-RIM:], axis, forward)  8.42 us
    pallas_call x1, Pallas kernels, shards(): pl.pallas_call(unwarp_kernel, out_shape=jax.ShapeDtypeStruct((rows, cols)...  8.19 us
  transfers between devices with their start and end apart: 5, of which 3 were waited for; matrix products, arithmetic and copies ran while one was open for 5% of the time, Pallas kernels for 0%

profile of v1, /device:TPU:11, one launch (start us, length us, event | category | flops | bytes accessed | tf_op | source)
XLA Modules:
  0.0 285.5 jit_solution(8596136679776066414)
XLA Ops:
  0.6 1.0 slice_bitcast_fusion
  1.6 2.6 collective-permute-start.1
  4.2 3.9 %collective-permute-start = (bf16[16,4096]{1,0:T(8,128)(2,1)S(1)}, bf16[16,4096]{1,0:T(8,128)(2,1)S(1)}, u32[]{:S(2)}, u32[]{:S(2)}) collective-permute-start(bf16[16,4096]{1,0:T(8,128)(2,1)S(1)} %get-tuple-element.9), channel_id=1, source_target_pairs={{0,1},{1,2},{2,3},{3,4},{4,5},{5,6},{6,7},{8,9},{9,10},{10,11},{11... | collective-permute-start | bytes 393224 | tf_op jit(solution)/shard_map/ppermute | solution.py:23
  8.5 1.6 iota_compare_fusion
  10.1 0.7 select_reduce_fusion.1
  10.8 4.6 %select_reduce_fusion.column_bands = bf16[3,512,256]{2,1,0:T(8,128)(2,1)} fusion(pred[21,512,256]{2,1,0:T(8,128)(4,1)S(1)} %iota_compare_fusion, bf16[3,21]{1,0:T(4,128)(2,1)S(1)} %copy-done.8), kind=kLoop, calls=%fused_computation | loop fusion | flops 16121856 | bytes 3539070 | tf_op jit(solution)/shard_map/reduce_sum | solution.py:37
  15.4 0.9 convert_reduce_fusion
  16.4 0.8 copy.14
  17.3 0.6 dynamic_slice.13.weight
  17.9 1.2 fusion.5
  19.8 27.4 %shard_map.113 = bf16[128,128,128]{2,1,0:T(8,128)(2,1)} custom-call(f32[1,3]{1,0:T(1,128)} %coef.3, s32[64]{0:T(128)} %get-tuple-element.10.ident, s32[64]{0:T(128)} %get-tuple-element.11.place, f32[1]{0:T(128)} %dynamic_slice.13.weight, bf16[16,4096]{1,0:T(8,128)(2,1)} %copy-done.2, bf16[256,4096]{1,0:T(8,128)(2,1)} %bitcast.21, ...), custom_call_target="tpu_custom_call" | custom-call | tf_op jit(solution)/shard_map/pallas_call | solution.py:259
  47.2 4.9 %all-to-all-start = ((bf16[32,4,128,128]{3,2,1,0:T(8,128)(2,1)}), bf16[32,4,128,128]{3,2,1,0:T(8,128)(2,1)}, u32[]{:S(2)}, u32[]{:S(2)}) async-start(bf16[32,4,128,128]{3,2,1,0:T(8,128)(2,1)} %bitcast.19), calls=%async_computation | async-start | bytes 8388608 | tf_op jit(solution)/shard_map/all_to_all | solution.py:271
  53.2 0.7 reshape.86.slot
  53.9 0.8 select_reduce_fusion.2
  55.2 87.9 %all-to-all-done = bf16[32,4,128,128]{3,2,1,0:T(8,128)(2,1)} async-done(((bf16[32,4,128,128]{3,2,1,0:T(8,128)(2,1)}), bf16[32,4,128,128]{3,2,1,0:T(8,128)(2,1)}, u32[]{:S(2)}, u32[]{:S(2)}) %all-to-all-start) | async-done | bytes 4194336 | tf_op jit(solution)/shard_map/all_to_all | solution.py:271
  143.1 10.9 %shard_map.114 = (f32[1024,1024]{1,0:T(8,128)}, bf16[128,128,128]{2,1,0:T(8,128)(2,1)}) custom-call(s32[128]{0:T(128)} %reshape.86.slot, s32[128]{0:T(128)} %reshape.93.valid, f32[64]{0:T(128)} %maximum_divide_fusion.inverse, bf16[128,128,128]{2,1,0:T(8,128)(2,1)} %bitcast.10.arrived), custom_call_target="tpu_custom_call" | custom-call | tf_op jit(solution)/shard_map/pallas_call | solution.py:272
  154.0 100.2 %all_to_all.10 = bf16[32,4,128,128]{3,2,1,0:T(8,128)(2,1)} all-to-all(bf16[32,4,128,128]{3,2,1,0:T(8,128)(2,1)} %bitcast.24), channel_id=1, replica_groups=mesh['exp'=4,'tile'=8] {'exp','tile'}, dimensions={0} | all-to-all | bytes 8388608 | tf_op jit(solution)/shard_map/all_to_all | solution.py:283
  254.2 8.2 %shard_map.115.image = bf16[256,4096]{1,0:T(8,128)(2,1)} custom-call(s32[64]{0:T(128)} %get-tuple-element.10.ident, s32[64]{0:T(128)} %get-tuple-element.11.place, bf16[128,128,128]{2,1,0:T(8,128)(2,1)} %bitcast.20, bf16[64,128,128]{2,1,0:T(8,128)(2,1)} %warp_rows.3, bf16[64,128,128]{2,1,0:T(8,128)(2,1)} %warp_columns.3), custom_call_target="tpu_custom_call" | custom-call | tf_op jit(solution)/shard_map/pallas_call | solution.py:284
  262.4 1.0 fusion.7
  263.4 1.9 collective-permute-start.3
  265.3 4.5 %collective-permute-start.2 = (bf16[16,4096]{1,0:T(8,128)(2,1)S(1)}, bf16[16,4096]{1,0:T(8,128)(2,1)S(1)}, u32[]{:S(2)}, u32[]{:S(2)}) collective-permute-start(bf16[16,4096]{1,0:T(8,128)(2,1)S(1)} %get-tuple-element.7), channel_id=1, source_target_pairs={{0,1},{1,2},{2,3},{3,4},{4,5},{5,6},{6,7},{8,9},{9,10},{10,11},{11... | collective-permute-start | bytes 393224 | tf_op jit(solution)/shard_map/ppermute | solution.py:23
  269.9 1.8 collective-permute-done.3.below
  272.3 0.6 copy-done.4
  272.9 12.6 %shard_map.116 = f32[256,4096]{1,0:T(8,128)} custom-call(f32[1,3]{1,0:T(1,128)} %coef.3, bf16[16,4096]{1,0:T(8,128)(2,1)} %copy-done.4, bf16[256,4096]{1,0:T(8,128)(2,1)} %shard_map.115.image, bf16[16,4096]{1,0:T(8,128)(2,1)} %copy-done.3, bf16[384,160]{1,0:T(8,128)(2,1)} %bitcast.26, bf16[3,512,256]{2,1,0:T(8,128)(2,1)} %select_reduce_fusion.column_bands, ...), custom_call_target="tpu_custom_call" | custom-call | tf_op jit(solution)/shard_map/pallas_call | solution.py:292
  (33 shorter events, 3.4 us)
Async XLA Ops:
  0.6 9.4 %copy-start.7 = (bf16[3,21]{1,0:T(4,128)(2,1)S(1)}, bf16[3,21]{1,0:T(4,128)(2,1)}, u32[]{:S(2)}) copy-start(bf16[3,21]{1,0:T(4,128)(2,1)} %param.11) | copy-start | bytes 382
  0.6 10.1 %copy-start.8 = (bf16[3,21]{1,0:T(4,128)(2,1)S(1)}, bf16[3,21]{1,0:T(4,128)(2,1)}, u32[]{:S(2)}) copy-start(bf16[3,21]{1,0:T(4,128)(2,1)} %param.12) | copy-start | bytes 382
  1.6 17.5 %collective-permute-start.1 = (bf16[16,4096]{1,0:T(8,128)(2,1)S(1)}, bf16[16,4096]{1,0:T(8,128)(2,1)S(1)}, u32[]{:S(2)}, u32[]{:S(2)}) collective-permute-start(bf16[16,4096]{1,0:T(8,128)(2,1)S(1)} %get-tuple-element.8), channel_id=1, source_target_pairs={{1,0},{2,1},{3,2},{4,3},{5,4},{6,5},{7,6},{9,8},{10,9},{11,10},{12... | collective-permute-start | bytes 393224 | tf_op jit(solution)/shard_map/ppermute | solution.py:24
  4.2 14.9 %collective-permute-start = (bf16[16,4096]{1,0:T(8,128)(2,1)S(1)}, bf16[16,4096]{1,0:T(8,128)(2,1)S(1)}, u32[]{:S(2)}, u32[]{:S(2)}) collective-permute-start(bf16[16,4096]{1,0:T(8,128)(2,1)S(1)} %get-tuple-element.9), channel_id=1, source_target_pairs={{0,1},{1,2},{2,3},{3,4},{4,5},{5,6},{6,7},{8,9},{9,10},{10,11},{11... | collective-permute-start | bytes 393224 | tf_op jit(solution)/shard_map/ppermute | solution.py:23
  10.0 5.4 %copy-start = (s32[4,8,64]{2,1,0:T(8,128)S(1)}, s32[4,8,64]{2,1,0:T(8,128)}, u32[]{:S(2)}) copy-start(s32[4,8,64]{2,1,0:T(8,128)} %param.17) | copy-start | bytes 24580
  10.1 6.3 %copy-start.6 = (f32[4,8]{1,0:T(4,128)S(1)}, f32[4,8]{1,0:T(4,128)}, u32[]{:S(2)}) copy-start(f32[4,8]{1,0:T(4,128)} %param.19) | copy-start | bytes 388
  19.1 0.6 copy-start.1
  19.1 0.7 copy-start.2
  47.2 5.8 %copy-start.5 = (s32[4,8,64]{2,1,0:T(8,128)S(1)}, s32[4,8,64]{2,1,0:T(8,128)}, u32[]{:S(2)}) copy-start(s32[4,8,64]{2,1,0:T(8,128)} %param.18) | copy-start | bytes 24580
  47.2 95.9 %all-to-all-start = ((bf16[32,4,128,128]{3,2,1,0:T(8,128)(2,1)}), bf16[32,4,128,128]{3,2,1,0:T(8,128)(2,1)}, u32[]{:S(2)}, u32[]{:S(2)}) async-start(bf16[32,4,128,128]{3,2,1,0:T(8,128)(2,1)} %bitcast.19), calls=%async_computation | async-start | bytes 8388608 | tf_op jit(solution)/shard_map/all_to_all | solution.py:271
  263.4 8.2 %collective-permute-start.3 = (bf16[16,4096]{1,0:T(8,128)(2,1)S(1)}, bf16[16,4096]{1,0:T(8,128)(2,1)S(1)}, u32[]{:S(2)}, u32[]{:S(2)}) collective-permute-start(bf16[16,4096]{1,0:T(8,128)(2,1)S(1)} %get-tuple-element.6), channel_id=1, source_target_pairs={{1,0},{2,1},{3,2},{4,3},{5,4},{6,5},{7,6},{9,8},{10,9},{11,10},{12... | collective-permute-start | bytes 393224 | tf_op jit(solution)/shard_map/ppermute | solution.py:24
  265.3 6.5 %collective-permute-start.2 = (bf16[16,4096]{1,0:T(8,128)(2,1)S(1)}, bf16[16,4096]{1,0:T(8,128)(2,1)S(1)}, u32[]{:S(2)}, u32[]{:S(2)}) collective-permute-start(bf16[16,4096]{1,0:T(8,128)(2,1)S(1)} %get-tuple-element.7), channel_id=1, source_target_pairs={{0,1},{1,2},{2,3},{3,4},{4,5},{5,6},{6,7},{8,9},{9,10},{10,11},{11... | collective-permute-start | bytes 393224 | tf_op jit(solution)/shard_map/ppermute | solution.py:23
  271.6 0.6 copy-start.3
  272.3 0.6 copy-start.4

commit v2 on v1

--- a/solution.py
+++ b/solution.py
@@ -25,19 +25,31 @@
     return above, below
 
 
-def banded(taps, rows, cols, offset, transposed):
+def banded(taps, rows, cols, offset):
     shape = (rows, cols)
     lag = lax.broadcasted_iota(jnp.int32, shape, 1) - lax.broadcasted_iota(jnp.int32, shape, 0)
     lag = lag - offset
-    if transposed:
-        lag = lag.T
     count = taps.shape[1]
-    hit = lag[None, :, :] == jnp.arange(count, dtype=jnp.int32)[:, None, None]
-    picked = jnp.where(hit[None], taps[:, :, None, None], jnp.zeros((), taps.dtype))
-    return jnp.sum(picked.astype(jnp.float32), axis=1).astype(jnp.bfloat16)
-
-
-def row_stage(coef, above, image, below, row_bands, padded, passes):
+    total = jnp.zeros((taps.shape[0], rows, cols), jnp.float32)
+    for tap in range(count):
+        value = taps[:, tap, None, None].astype(jnp.float32)
+        total = total + jnp.where(lag == tap, value, 0.0)
+    return total.astype(jnp.bfloat16)
+
+
+def banded_transposed(taps, rows, cols, offset):
+    shape = (rows, cols)
+    lag = lax.broadcasted_iota(jnp.int32, shape, 0) - lax.broadcasted_iota(jnp.int32, shape, 1)
+    lag = lag - offset
+    count = taps.shape[1]
+    total = jnp.zeros((taps.shape[0], rows, cols), jnp.float32)
+    for tap in range(count):
+        value = taps[:, tap, None, None].astype(jnp.float32)
+        total = total + jnp.where(lag == tap, value, 0.0)
+    return total.astype(jnp.bfloat16)
+
+
+def row_stage(coef, above, image, below, row_bands, column_bands, padded, passes, bands):
     bases = passes.shape[0]
     rows, cols = image.shape
     blocks = rows // BLOCK
@@ -46,6 +58,10 @@
     padded[RIM : RIM + rows, :] = image[...]
     padded[RIM + rows :, :] = below[...]
     edge = jnp.zeros((rows, BLOCK), passes.dtype)
+    bands[...] = jnp.zeros_like(bands)
+    for side in range(WIDE // BLOCK):
+        top = side * BLOCK
+        bands[:, top : top + 3 * BLOCK, top : top + BLOCK] = column_bands[...]
     for basis in range(bases):
         passes[basis, :, :BLOCK] = edge
         passes[basis, :, BLOCK + cols :] = edge
@@ -81,46 +97,166 @@
     return total
 
 
-def forward_kernel(
-    coef, ident, place, weight, above, image, below, row_bands, column_bands, warp_rows,
-    warp_columns, packed, padded, passes,
+def match_kernel(
+    coef, above, image, below, row_bands, column_bands, matched, padded, passes, bands
 ):
     rows, cols = image.shape
     blocks = rows // BLOCK
     across = cols // BLOCK
-    row_stage(coef, above, image, below, row_bands, padded, passes)
-    blank = jnp.zeros((BLOCK, BLOCK), packed.dtype)
-
-    def clear(at, carry):
-        packed[at] = blank
-        return carry
-
-    lax.fori_loop(0, packed.shape[0], clear, 0, unroll=4)
-    scale = weight[0]
+    row_stage(coef, above, image, below, row_bands, column_bands, padded, passes, bands)
+    matched[blocks * across] = jnp.zeros((BLOCK, BLOCK), matched.dtype)
 
     def step(at, carry):
         start = pl.multiple_of(at * WIDE, WIDE)
-        matched = column_chunk(passes, column_bands, start).astype(jnp.bfloat16)
+        chunk = column_chunk(passes, bands, start).astype(matched.dtype)
         for block in range(blocks):
             for side in range(WIDE // BLOCK):
                 number = block * across + at * (WIDE // BLOCK) + side
-                which = ident[number]
-                piece = matched[
+                matched[number] = chunk[
                     block * BLOCK : (block + 1) * BLOCK, side * BLOCK : (side + 1) * BLOCK
                 ]
-                first = jnp.dot(
-                    warp_rows[which], piece, preferred_element_type=jnp.float32
-                ).astype(jnp.bfloat16)
-                second = lax.dot_general(
-                    first,
-                    warp_columns[which],
-                    (((1,), (1,)), ((), ())),
-                    preferred_element_type=jnp.float32,
-                )
-                packed[place[number]] = (scale * second).astype(packed.dtype)
         return carry
 
     lax.fori_loop(0, cols // WIDE, step, 0, unroll=2)
+
+
+def partner(me, step, devices):
+    sign = 2 * lax.rem(step, 2) - 1
+    shift = devices // 2 + sign * lax.div(step + 1, 2)
+    return lax.rem(me + shift, devices), lax.rem(me + devices - shift, devices)
+
+
+def address(device, n_tile):
+    return (lax.div(device, n_tile), lax.rem(device, n_tile))
+
+
+def greet(me, devices, n_tile):
+    barrier = pltpu.get_barrier_semaphore()
+
+    def hello(step, carry):
+        other = lax.rem(me + step + 1, devices)
+        pl.semaphore_signal(
+            barrier, inc=1, device_id=address(other, n_tile), device_id_type=pl.DeviceIdType.MESH
+        )
+        return carry
+
+    lax.fori_loop(0, devices - 1, hello, 0)
+    pl.semaphore_wait(barrier, devices - 1)
+
+
+def transfer(source, target, me, other, capacity, n_tile, send_sem, recv_sem):
+    return pltpu.make_async_remote_copy(
+        src_ref=source.at[pl.ds(other * capacity, capacity)],
+        dst_ref=target.at[pl.ds(me * capacity, capacity)],
+        send_sem=send_sem.at[other],
+        recv_sem=recv_sem.at[me],
+        device_id=address(other, n_tile),
+        device_id_type=pl.DeviceIdType.MESH,
+    )
+
+
+def receipt(source, target, other, capacity, n_tile, send_sem, recv_sem):
+    return pltpu.make_async_remote_copy(
+        src_ref=source.at[pl.ds(other * capacity, capacity)],
+        dst_ref=target.at[pl.ds(other * capacity, capacity)],
+        send_sem=send_sem.at[other],
+        recv_sem=recv_sem.at[other],
+        device_id=address(other, n_tile),
+        device_id_type=pl.DeviceIdType.MESH,
+    )
+
+
+def send_kernel(
+    n_exp, n_tile, source, ident, weight, matched, warp_rows, warp_columns, arrived, packed,
+    send_sem, recv_sem,
+):
+    devices = n_exp * n_tile
+    capacity = packed.shape[0] // devices
+    me = lax.axis_index("exp") * n_tile + lax.axis_index("tile")
+    greet(me, devices, n_tile)
+    scale = weight[0]
+
+    def warp(other, target):
+        for rank in range(capacity):
+            spot = other * capacity + rank
+            which = ident[spot]
+            first = jnp.dot(
+                warp_rows[which], matched[source[spot]], preferred_element_type=jnp.float32
+            ).astype(jnp.bfloat16)
+            second = lax.dot_general(
+                first,
+                warp_columns[which],
+                (((1,), (1,)), ((), ())),
+                preferred_element_type=jnp.float32,
+            )
+            target[spot] = (scale * second).astype(target.dtype)
+
+    def step(at, carry):
+        other, _ = partner(me, at, devices)
+        warp(other, packed)
+        transfer(packed, arrived, me, other, capacity, n_tile, send_sem, recv_sem).start()
+        return carry
+
+    lax.fori_loop(0, devices - 1, step, 0)
+    warp(me, arrived)
+
+    def finish(at, carry):
+        _, other = partner(me, at, devices)
+        receipt(packed, arrived, other, capacity, n_tile, send_sem, recv_sem).wait()
+        return carry
+
+    lax.fori_loop(0, devices - 1, finish, 0)
+
+
+def return_kernel(
+    n_exp, n_tile, ident, place, picked, warp_rows, warp_columns, image, returned, unwarped,
+    send_sem, recv_sem,
+):
+    devices = n_exp * n_tile
+    capacity = picked.shape[0] // devices
+    across = image.shape[1] // BLOCK
+    me = lax.axis_index("exp") * n_tile + lax.axis_index("tile")
+    greet(me, devices, n_tile)
+
+    def begin(at, carry):
+        other, _ = partner(me, at, devices)
+        transfer(picked, returned, me, other, capacity, n_tile, send_sem, recv_sem).start()
+        return carry
+
+    lax.fori_loop(0, devices - 1, begin, 0)
+
+    def unwarp(other, origin):
+        for rank in range(capacity):
+            spot = other * capacity + rank
+            which = ident[spot]
+            back = lax.dot_general(
+                warp_rows[which],
+                origin[spot],
+                (((0,), (0,)), ((), ())),
+                preferred_element_type=jnp.float32,
+            ).astype(jnp.bfloat16)
+            piece = jnp.dot(back, warp_columns[which], preferred_element_type=jnp.float32)
+            unwarped[spot] = piece.astype(unwarped.dtype)
+
+    unwarp(me, picked)
+
+    def finish(at, carry):
+        _, other = partner(me, at, devices)
+        receipt(picked, returned, other, capacity, n_tile, send_sem, recv_sem).wait()
+        unwarp(other, returned)
+        return carry
+
+    lax.fori_loop(0, devices - 1, finish, 0)
+
+    def gather(at, carry):
+        left = pl.multiple_of(at * BLOCK, BLOCK)
+        for block in range(image.shape[0] // BLOCK):
+            image[block * BLOCK : (block + 1) * BLOCK, pl.ds(left, BLOCK)] = unwarped[
+                place[block * across + at]
+            ]
+        return carry
+
+    lax.fori_loop(0, across, gather, 0)
 
 
 def coadd_kernel(slot, valid, inverse, arrived, patch, picked):
@@ -158,41 +294,16 @@
     lax.fori_loop(0, arrived.shape[0], pick, 0, unroll=4)
 
 
-def unwarp_kernel(ident, place, returned, warp_rows, warp_columns, image):
-    rows, cols = image.shape
-    blocks = rows // BLOCK
-    across = cols // BLOCK
+def difference_kernel(
+    coef, above, image, below, row_bands, column_bands, exposure, difference, padded, passes,
+    bands,
+):
+    cols = image.shape[1]
+    row_stage(coef, above, image, below, row_bands, column_bands, padded, passes, bands)
 
     def step(at, carry):
         start = pl.multiple_of(at * WIDE, WIDE)
-        for block in range(blocks):
-            for side in range(WIDE // BLOCK):
-                number = block * across + at * (WIDE // BLOCK) + side
-                which = ident[number]
-                back = lax.dot_general(
-                    warp_rows[which],
-                    returned[place[number]],
-                    (((0,), (0,)), ((), ())),
-                    preferred_element_type=jnp.float32,
-                ).astype(jnp.bfloat16)
-                piece = jnp.dot(back, warp_columns[which], preferred_element_type=jnp.float32)
-                image[
-                    block * BLOCK : (block + 1) * BLOCK, pl.ds(start + side * BLOCK, BLOCK)
-                ] = piece.astype(image.dtype)
-        return carry
-
-    lax.fori_loop(0, cols // WIDE, step, 0, unroll=2)
-
-
-def difference_kernel(
-    coef, above, image, below, row_bands, column_bands, exposure, difference, padded, passes
-):
-    cols = image.shape[1]
-    row_stage(coef, above, image, below, row_bands, padded, passes)
-
-    def step(at, carry):
-        start = pl.multiple_of(at * WIDE, WIDE)
-        matched = column_chunk(passes, column_bands, start)
+        matched = column_chunk(passes, bands, start)
         spot = pl.ds(start, WIDE)
         difference[:, spot] = exposure[:, spot].astype(jnp.float32) - matched
         return carry
@@ -226,9 +337,9 @@
     mine = exposure[0]
 
     above, below = halo(mine, "tile")
-    row_bands = banded(row_taps, BLOCK, BLOCK + 2 * RIM, RIM - HALF, False)
+    row_bands = banded(row_taps, BLOCK, BLOCK + 2 * RIM, RIM - HALF)
     row_bands = row_bands.reshape(bases * BLOCK, BLOCK + 2 * RIM)
-    column_bands = banded(column_taps, WIDE, 2 * WIDE, BLOCK - HALF, True)
+    column_bands = banded_transposed(column_taps, 3 * BLOCK, BLOCK, BLOCK - HALF)
 
     dest_all = route_device.reshape(devices, blocks)
     slot_all = route_slot.reshape(devices, blocks)
@@ -239,6 +350,11 @@
     place_all = dest_all * capacity + rank_all
     place = lax.dynamic_index_in_dim(place_all, myself, 0, keepdims=False)
     ident = lax.dynamic_index_in_dim(warp_id.reshape(devices, blocks), myself, 0, keepdims=False)
+    taken = place[None, :] == jnp.arange(buffered, dtype=jnp.int32)[:, None]
+    source = jnp.min(
+        jnp.where(taken, jnp.arange(blocks, dtype=jnp.int32)[None, :], blocks), axis=1
+    )
+    spot_ident = jnp.sum(jnp.where(taken, ident[None, :], 0), axis=1, dtype=jnp.int32)
     my_weight = lax.dynamic_index_in_dim(weight_all, myself, 0, keepdims=True)
     hit = (dest_all[:, None, :] == myself) & (
         rank_all[:, None, :] == jnp.arange(capacity, dtype=jnp.int32)[None, :, None]
@@ -255,39 +371,48 @@
     work = [
         pltpu.VMEM((rows + 2 * RIM, cols), jnp.bfloat16),
         pltpu.VMEM((bases, rows, cols + 2 * BLOCK), jnp.bfloat16),
+        pltpu.VMEM((bases, 2 * WIDE, WIDE), jnp.bfloat16),
     ]
-    packed = pl.pallas_call(
-        forward_kernel,
-        out_shape=jax.ShapeDtypeStruct((buffered, BLOCK, BLOCK), jnp.bfloat16),
-        in_specs=scalars(4) + vectors(7),
+    semaphores = [pltpu.SemaphoreType.DMA((devices,)), pltpu.SemaphoreType.DMA((devices,))]
+    buffer = jax.ShapeDtypeStruct((buffered, BLOCK, BLOCK), jnp.bfloat16)
+    matched = pl.pallas_call(
+        match_kernel,
+        out_shape=jax.ShapeDtypeStruct((blocks + 1, BLOCK, BLOCK), jnp.bfloat16),
+        in_specs=scalars(1) + vectors(5),
         out_specs=pl.BlockSpec(memory_space=pltpu.VMEM),
         scratch_shapes=work,
         compiler_params=params,
-    )(
-        basis_coef, ident, place, my_weight, above, mine, below, row_bands, column_bands,
-        warp_rows, warp_columns,
-    )
-    packed = packed.reshape(devices, capacity, BLOCK, BLOCK)
-    arrived = lax.all_to_all(packed, ("exp", "tile"), split_axis=0, concat_axis=0, tiled=True)
+    )(basis_coef, above, mine, below, row_bands, column_bands)
+    arrived = pl.pallas_call(
+        functools.partial(send_kernel, n_exp, n_tile),
+        out_shape=buffer,
+        in_specs=scalars(3) + vectors(3),
+        out_specs=pl.BlockSpec(memory_space=pltpu.VMEM),
+        scratch_shapes=[pltpu.VMEM(buffer.shape, buffer.dtype)] + semaphores,
+        compiler_params=pltpu.CompilerParams(
+            vmem_limit_bytes=VMEM_BYTES, collective_id=0, has_side_effects=True
+        ),
+    )(source, spot_ident, my_weight, matched, warp_rows, warp_columns)
     patch, picked = pl.pallas_call(
         coadd_kernel,
         out_shape=(
             jax.ShapeDtypeStruct((SLOT_ROWS * BLOCK, SLOT_COLS * BLOCK), jnp.float32),
-            jax.ShapeDtypeStruct((buffered, BLOCK, BLOCK), jnp.bfloat16),
+            buffer,
         ),
         in_specs=scalars(3) + vectors(1),
         out_specs=tuple(vectors(2)),
         compiler_params=params,
-    )(slot, valid, inverse, arrived.reshape(buffered, BLOCK, BLOCK))
-    picked = picked.reshape(devices, capacity, BLOCK, BLOCK)
-    returned = lax.all_to_all(picked, ("exp", "tile"), split_axis=0, concat_axis=0, tiled=True)
+    )(slot, valid, inverse, arrived)
     template = pl.pallas_call(
-        unwarp_kernel,
+        functools.partial(return_kernel, n_exp, n_tile),
         out_shape=jax.ShapeDtypeStruct((rows, cols), jnp.bfloat16),
         in_specs=scalars(2) + vectors(3),
         out_specs=pl.BlockSpec(memory_space=pltpu.VMEM),
-        compiler_params=params,
-    )(ident, place, returned.reshape(buffered, BLOCK, BLOCK), warp_rows, warp_columns)
+        scratch_shapes=[pltpu.VMEM(buffer.shape, buffer.dtype)] * 2 + semaphores,
+        compiler_params=pltpu.CompilerParams(
+            vmem_limit_bytes=VMEM_BYTES, collective_id=1, has_side_effects=True
+        ),
+    )(spot_ident, place, picked, warp_rows, warp_columns)
     template_above, template_below = halo(template, "tile")
     difference = pl.pallas_call(
         difference_kernel,

time: 287 us -> 289 us (level)
  Pallas kernels: 59.1 us -> 251 us
  blocking collectives: 100 us -> 0 us
  waiting for transfers between devices: 89.8 us -> 1.93 us
  starting transfers between devices: 17.8 us -> 12.9 us
  other arithmetic: 10.9 us -> 14.4 us
    pallas_call x2 -> x3, Pallas kernels: 35.6 us -> 227 us  [the longest x1 114 us: shards(): pl.pallas_call(functools.partial(return_kernel, n_exp, n_tile), out_shape...]
    all_to_all x1 -> x0, blocking collectives: 100 us -> none  [shards(): lax.all_to_all(picked, ('exp', 'tile'), split_axis=0, concat_axis=0, tile...]
    all_to_all x1 -> x0, waiting for transfers between devices: 87.9 us -> none  [shards(): lax.all_to_all(packed, ('exp', 'tile'), split_axis=0, concat_axis=0, tile...]
    convert_element_type x0 -> x6, other arithmetic: none -> 9.82 us  [the longest x2 2.87 us: banded_transposed(): value = taps[:, tap, None, None].astype(jnp.float32)]
    all_to_all x1 -> x0, starting transfers between devices: 4.87 us -> none  [shards(): lax.all_to_all(packed, ('exp', 'tile'), split_axis=0, concat_axis=0, tile...]
    reduce_sum x2 -> x1, other arithmetic: 5.31 us -> 0.66 us  [shards(): jnp.sum(jnp.where(taken, ident[None, :], 0), axis=1, dtype=jnp.int32)]
  transfers between devices with their start and end apart: 5 -> 4, of which waited for: 3 -> 2; matrix products, arithmetic and copies ran while one was open for 5% -> 6% of each run, Pallas kernels for 0% -> 0%
where the time goes in v2:
time: 289 us; the launch traced here: 287 us
  Pallas kernels  251 us (87%)
  other arithmetic  14.4 us (5%)
  starting transfers between devices  12.9 us (4%)
  local copies, waits for them, and re-layouts  6.32 us (2%)
    pallas_call x1, Pallas kernels, shards(): pl.pallas_call(functools.partial(return_kernel, n_exp, n_tile), out_shape...  114 us
    pallas_call x1, Pallas kernels, shards(): pl.pallas_call(functools.partial(send_kernel, n_exp, n_tile), out_shape=b...  102 us
    pallas_call x1, Pallas kernels, shards(): pl.pallas_call(difference_kernel, out_shape=jax.ShapeDtypeStruct((rows, c...  12.6 us
    pallas_call x1, Pallas kernels, shards(): pl.pallas_call(coadd_kernel, out_shape=(jax.ShapeDtypeStruct((SLOT_ROWS *...  11.1 us
    pallas_call x1, Pallas kernels, shards(): pl.pallas_call(match_kernel, out_shape=jax.ShapeDtypeStruct((blocks + 1,...  11 us
    ppermute x2, starting transfers between devices, halo(): above = lax.ppermute(image[-RIM:], axis, forward)  6.82 us
    ppermute x2, starting transfers between devices, halo(): below = lax.ppermute(image[:RIM], axis, backward)  6.1 us
  transfers between devices with their start and end apart: 4, of which 2 were waited for; matrix products, arithmetic and copies ran while one was open for 6% of the time, Pallas kernels for 0%

profile of v2, /device:TPU:11, one launch (start us, length us, event | category | flops | bytes accessed | tf_op | source)
XLA Modules:
  0.0 287.3 jit_solution(15328360607761350991)
XLA Ops:
  0.7 1.0 slice_bitcast_fusion
  1.7 2.6 collective-permute-start.1
  4.3 3.9 %collective-permute-start = (bf16[16,4096]{1,0:T(8,128)(2,1)S(1)}, bf16[16,4096]{1,0:T(8,128)(2,1)S(1)}, u32[]{:S(2)}, u32[]{:S(2)}) collective-permute-start(bf16[16,4096]{1,0:T(8,128)(2,1)S(1)} %get-tuple-element.53), channel_id=1, source_target_pairs={{0,1},{1,2},{2,3},{3,4},{4,5},{5,6},{6,7},{8,9},{9,10},{10,11},{11... | collective-permute-start | bytes 393224 | tf_op jit(solution)/shard_map/ppermute | solution.py:23
  8.2 1.0 convert_reduce_fusion.23
  9.1 1.9 convert_reduce_fusion.42
  11.0 1.0 convert_reduce_fusion.2
  12.0 1.9 convert_reduce_fusion.21
  14.9 0.9 convert_reduce_fusion
  16.1 0.8 select_reduce_fusion
  18.2 1.9 add_convert_fusion.column_bands
  20.1 0.7 fusion.47
  21.5 0.7 reshape.470.valid
  22.2 0.7 reshape.468.slot
  22.9 2.2 add_convert_fusion.1.row_bands
  26.5 11.0 %shard_map.113.matched = bf16[65,128,128]{2,1,0:T(8,128)(2,1)} custom-call(f32[1,3]{1,0:T(1,128)} %coef.3, bf16[16,4096]{1,0:T(8,128)(2,1)} %copy-done.4, bf16[256,4096]{1,0:T(8,128)(2,1)} %bitcast.98, bf16[16,4096]{1,0:T(8,128)(2,1)} %copy-done.3, bf16[384,160]{1,0:T(8,128)(2,1)} %add_convert_fusion.1.row_bands, ...), custom_call_target="tpu_custom_call" | custom-call | tf_op jit(solution)/shard_map/pallas_call | solution.py:378
  37.4 102.3 %shard_map.114.arrived = bf16[128,128,128]{2,1,0:T(8,128)(2,1)} custom-call(s32[128]{0:T(128)} %get-tuple-element.49.source, s32[128]{0:T(128)} %get-tuple-element.48.ident, f32[1]{0:T(128)} %dynamic_slice.13.weight, bf16[65,128,128]{2,1,0:T(8,128)(2,1)} %shard_map.113.matched, bf16[64,128,128]{2,1,0:T(8,128)(2,1)} %warp_rows.3, ...), custom_call_target="tpu_custom_call" | custom-call | tf_op jit(solution)/shard_map/pallas_call | solution.py:386
  139.7 11.1 %shard_map.115 = (f32[1024,1024]{1,0:T(8,128)}, bf16[128,128,128]{2,1,0:T(8,128)(2,1)}) custom-call(s32[128]{0:T(128)} %reshape.468.slot, s32[128]{0:T(128)} %reshape.470.valid, f32[64]{0:T(128)} %maximum_divide_fusion.inverse, bf16[128,128,128]{2,1,0:T(8,128)(2,1)} %shard_map.114.arrived), custom_call_target="tpu_custom_call" | custom-call | tf_op jit(solution)/shard_map/pallas_call | solution.py:396
  150.9 113.8 %shard_map.116.image = bf16[256,4096]{1,0:T(8,128)(2,1)} custom-call(s32[128]{0:T(128)} %get-tuple-element.48.ident, s32[64]{0:T(128)} %copy-done.6, bf16[128,128,128]{2,1,0:T(8,128)(2,1)} %get-tuple-element.5.picked, bf16[64,128,128]{2,1,0:T(8,128)(2,1)} %warp_rows.3, bf16[64,128,128]{2,1,0:T(8,128)(2,1)} %warp_columns.3), custom_call_target="tpu_custom_call" | custom-call | tf_op jit(solution)/shard_map/pallas_call | solution.py:406
  264.7 1.0 fusion.49
  265.7 3.5 %collective-permute-start.3 = (bf16[16,4096]{1,0:T(8,128)(2,1)S(1)}, bf16[16,4096]{1,0:T(8,128)(2,1)S(1)}, u32[]{:S(2)}, u32[]{:S(2)}) collective-permute-start(bf16[16,4096]{1,0:T(8,128)(2,1)S(1)} %get-tuple-element.50), channel_id=1, source_target_pairs={{1,0},{2,1},{3,2},{4,3},{5,4},{6,5},{7,6},{9,8},{10,9},{11,10},{12... | collective-permute-start | bytes 393224 | tf_op jit(solution)/shard_map/ppermute | solution.py:24
  269.2 2.9 %collective-permute-start.2 = (bf16[16,4096]{1,0:T(8,128)(2,1)S(1)}, bf16[16,4096]{1,0:T(8,128)(2,1)S(1)}, u32[]{:S(2)}, u32[]{:S(2)}) collective-permute-start(bf16[16,4096]{1,0:T(8,128)(2,1)S(1)} %get-tuple-element.51), channel_id=1, source_target_pairs={{0,1},{1,2},{2,3},{3,4},{4,5},{5,6},{6,7},{8,9},{9,10},{10,11},{11... | collective-permute-start | bytes 393224 | tf_op jit(solution)/shard_map/ppermute | solution.py:23
  272.1 0.7 collective-permute-done.3.below
  272.8 1.2 collective-permute-done.2.above
  274.7 12.6 %shard_map.117 = f32[256,4096]{1,0:T(8,128)} custom-call(f32[1,3]{1,0:T(1,128)} %coef.3, bf16[16,4096]{1,0:T(8,128)(2,1)} %copy-done.2, bf16[256,4096]{1,0:T(8,128)(2,1)} %shard_map.116.image, bf16[16,4096]{1,0:T(8,128)(2,1)} %copy-done.1, bf16[384,160]{1,0:T(8,128)(2,1)} %add_convert_fusion.1.row_bands, bf16[3,384,128]{2,1,0:T(8,128)(2,1)} %add_convert_fusion.column_bands, ...), custom_call_target="tpu_custom_call" | custom-call | tf_op jit(solution)/shard_map/pallas_call | solution.py:417
  (62 shorter events, 5.2 us)
Async XLA Ops:
  0.6 14.2 %copy-start.7 = (f32[4,8]{1,0:T(4,128)S(1)}, f32[4,8]{1,0:T(4,128)}, u32[]{:S(2)}) copy-start(f32[4,8]{1,0:T(4,128)} %param.19) | copy-start | bytes 388
  0.6 14.2 %copy-start = (s32[4,8,64]{2,1,0:T(8,128)S(1)}, s32[4,8,64]{2,1,0:T(8,128)}, u32[]{:S(2)}) copy-start(s32[4,8,64]{2,1,0:T(8,128)} %param.17) | copy-start | bytes 24580
  0.7 15.3 %copy-start.5 = (s32[4,8,64]{2,1,0:T(8,128)S(1)}, s32[4,8,64]{2,1,0:T(8,128)}, u32[]{:S(2)}) copy-start(s32[4,8,64]{2,1,0:T(8,128)} %param.18) | copy-start | bytes 24580
  1.7 24.1 %collective-permute-start.1 = (bf16[16,4096]{1,0:T(8,128)(2,1)S(1)}, bf16[16,4096]{1,0:T(8,128)(2,1)S(1)}, u32[]{:S(2)}, u32[]{:S(2)}) collective-permute-start(bf16[16,4096]{1,0:T(8,128)(2,1)S(1)} %get-tuple-element.52), channel_id=1, source_target_pairs={{1,0},{2,1},{3,2},{4,3},{5,4},{6,5},{7,6},{9,8},{10,9},{11,10},{12... | collective-permute-start | bytes 393224 | tf_op jit(solution)/shard_map/ppermute | solution.py:24
  4.3 21.5 %collective-permute-start = (bf16[16,4096]{1,0:T(8,128)(2,1)S(1)}, bf16[16,4096]{1,0:T(8,128)(2,1)S(1)}, u32[]{:S(2)}, u32[]{:S(2)}) collective-permute-start(bf16[16,4096]{1,0:T(8,128)(2,1)S(1)} %get-tuple-element.53), channel_id=1, source_target_pairs={{0,1},{1,2},{2,3},{3,4},{4,5},{5,6},{6,7},{8,9},{9,10},{10,11},{11... | collective-permute-start | bytes 393224 | tf_op jit(solution)/shard_map/ppermute | solution.py:23
  20.8 16.6 %copy-start.6 = (s32[64]{0:T(128)}, s32[64]{0:T(128)S(1)}, u32[]{:S(2)}) copy-start(s32[64]{0:T(128)S(1)} %get-tuple-element.55.place) | copy-start | bytes 772
  25.8 0.6 copy-start.3
  25.8 0.7 copy-start.4
  265.7 7.2 %collective-permute-start.3 = (bf16[16,4096]{1,0:T(8,128)(2,1)S(1)}, bf16[16,4096]{1,0:T(8,128)(2,1)S(1)}, u32[]{:S(2)}, u32[]{:S(2)}) collective-permute-start(bf16[16,4096]{1,0:T(8,128)(2,1)S(1)} %get-tuple-element.50), channel_id=1, source_target_pairs={{1,0},{2,1},{3,2},{4,3},{5,4},{6,5},{7,6},{9,8},{10,9},{11,10},{12... | collective-permute-start | bytes 393224 | tf_op jit(solution)/shard_map/ppermute | solution.py:24
  269.2 4.9 %collective-permute-start.2 = (bf16[16,4096]{1,0:T(8,128)(2,1)S(1)}, bf16[16,4096]{1,0:T(8,128)(2,1)S(1)}, u32[]{:S(2)}, u32[]{:S(2)}) collective-permute-start(bf16[16,4096]{1,0:T(8,128)(2,1)S(1)} %get-tuple-element.51), channel_id=1, source_target_pairs={{0,1},{1,2},{2,3},{3,4},{4,5},{5,6},{6,7},{8,9},{9,10},{10,11},{11... | collective-permute-start | bytes 393224 | tf_op jit(solution)/shard_map/ppermute | solution.py:23
  272.8 1.2 copy-start.1
  274.1 0.7 copy-start.2

commit v3 on v2

--- a/solution.py
+++ b/solution.py
@@ -98,9 +98,32 @@
 
 
 def match_kernel(
-    coef, above, image, below, row_bands, column_bands, matched, padded, passes, bands
+    capacity, coef, route, warp_id, above, image, below, row_bands, column_bands, matched, place,
+    source, ident, padded, passes, bands, count,
 ):
     rows, cols = image.shape
+    me = lax.axis_index("exp") * lax.axis_size("tile") + lax.axis_index("tile")
+
+    def clear(at, carry):
+        count[at] = 0
+        for rank in range(capacity):
+            source[at * capacity + rank] = route.shape[1]
+            ident[at * capacity + rank] = 0
+        return carry
+
+    lax.fori_loop(0, route.shape[0], clear, 0)
+
+    def assign(at, carry):
+        device = route[me, at]
+        rank = count[device]
+        count[device] = rank + 1
+        spot = device * capacity + rank
+        place[at] = spot
+        source[spot] = at
+        ident[spot] = warp_id[me, at]
+        return carry
+
+    lax.fori_loop(0, route.shape[1], assign, 0)
     blocks = rows // BLOCK
     across = cols // BLOCK
     row_stage(coef, above, image, below, row_bands, column_bands, padded, passes, bands)
@@ -121,8 +144,13 @@
 
 
 def partner(me, step, devices):
-    sign = 2 * lax.rem(step, 2) - 1
-    shift = devices // 2 + sign * lax.div(step + 1, 2)
+    half = devices // 2
+    pair = lax.div(step, 2)
+    odd = lax.rem(pair, 2)
+    far = half + (2 * odd - 1) * lax.div(pair + 1, 2)
+    near = (1 - odd) * (1 + lax.div(pair, 2)) + odd * (devices - 1 - lax.div(pair, 2))
+    turn = lax.rem(step, 2)
+    shift = (1 - turn) * far + turn * near
     return lax.rem(me + shift, devices), lax.rem(me + devices - shift, devices)
 
 
@@ -167,14 +195,14 @@
 
 
 def send_kernel(
-    n_exp, n_tile, source, ident, weight, matched, warp_rows, warp_columns, arrived, packed,
-    send_sem, recv_sem,
+    n_exp, n_tile, source, ident, weight, matched, warp_rows, warp_columns, route, slot, arrived,
+    table, packed, send_sem, recv_sem,
 ):
     devices = n_exp * n_tile
     capacity = packed.shape[0] // devices
     me = lax.axis_index("exp") * n_tile + lax.axis_index("tile")
     greet(me, devices, n_tile)
-    scale = weight[0]
+    scale = weight[lax.axis_index("exp"), lax.axis_index("tile")]
 
     def warp(other, target):
         for rank in range(capacity):
@@ -200,6 +228,24 @@
     lax.fori_loop(0, devices - 1, step, 0)
     warp(me, arrived)
 
+    count = route.shape[1]
+    hit = route[...] == me
+    later = (
+        lax.broadcasted_iota(jnp.int32, (count, count), 0)
+        < lax.broadcasted_iota(jnp.int32, (count, count), 1)
+    )
+    rank_of = jnp.dot(
+        hit.astype(jnp.float32), later.astype(jnp.float32), preferred_element_type=jnp.float32
+    ).astype(jnp.int32)
+    column = lax.broadcasted_iota(jnp.int32, table.shape, 1)
+    filled = jnp.zeros(table.shape, jnp.int32)
+    none = SLOT_ROWS * SLOT_COLS
+    for rank in range(capacity):
+        chosen = jnp.where(hit & (rank_of == rank), slot[...] - none, 0)
+        found = jnp.sum(chosen, axis=1, keepdims=True) + none
+        filled = jnp.where(column == rank, found, filled)
+    table[...] = filled
+
     def finish(at, carry):
         _, other = partner(me, at, devices)
         receipt(packed, arrived, other, capacity, n_tile, send_sem, recv_sem).wait()
@@ -209,8 +255,8 @@
 
 
 def return_kernel(
-    n_exp, n_tile, ident, place, picked, warp_rows, warp_columns, image, returned, unwarped,
-    send_sem, recv_sem,
+    n_exp, n_tile, ident, place, table, value, warp_rows, warp_columns, image, picked, returned,
+    unwarped, send_sem, recv_sem,
 ):
     devices = n_exp * n_tile
     capacity = picked.shape[0] // devices
@@ -218,8 +264,13 @@
     me = lax.axis_index("exp") * n_tile + lax.axis_index("tile")
     greet(me, devices, n_tile)
 
+    def pick(other):
+        for rank in range(capacity):
+            picked[other * capacity + rank] = value[table[other, rank]]
+
     def begin(at, carry):
         other, _ = partner(me, at, devices)
+        pick(other)
         transfer(picked, returned, me, other, capacity, n_tile, send_sem, recv_sem).start()
         return carry
 
@@ -238,6 +289,7 @@
             piece = jnp.dot(back, warp_columns[which], preferred_element_type=jnp.float32)
             unwarped[spot] = piece.astype(unwarped.dtype)
 
+    pick(me)
     unwarp(me, picked)
 
     def finish(at, carry):
@@ -259,39 +311,42 @@
     lax.fori_loop(0, across, gather, 0)
 
 
-def coadd_kernel(slot, valid, inverse, arrived, patch, picked):
-    side = SLOT_COLS * BLOCK
-    blank = jnp.zeros((BLOCK, side), jnp.float32)
-    for row in range(SLOT_ROWS):
-        patch[row * BLOCK : (row + 1) * BLOCK, :] = blank
-
-    def where(number):
-        top = pl.multiple_of((number // SLOT_COLS) * BLOCK, BLOCK)
-        left = pl.multiple_of((number % SLOT_COLS) * BLOCK, BLOCK)
-        return pl.ds(top, BLOCK), pl.ds(left, BLOCK)
+def coadd_kernel(n_tile, table, weight, arrived, patch, value, sums, total):
+    slots = SLOT_ROWS * SLOT_COLS
+    capacity = arrived.shape[0] // table.shape[0]
+    blank = jnp.zeros((BLOCK, BLOCK), jnp.float32)
+
+    def clear(at, carry):
+        sums[at] = blank
+        total[at] = 0.0
+        return carry
+
+    lax.fori_loop(0, slots + 1, clear, 0, unroll=5)
 
     def add(at, carry):
-        @pl.when(valid[at] != 0)
-        def _():
-            spot = where(slot[at])
-            patch[spot] = patch[spot] + arrived[at].astype(jnp.float32)
-
-        return carry
-
-    lax.fori_loop(0, arrived.shape[0], add, 0)
+        share = weight[lax.div(at, n_tile), lax.rem(at, n_tile)]
+        for rank in range(capacity):
+            slot = table[at, rank]
+            sums[slot] = sums[slot] + arrived[at * capacity + rank].astype(jnp.float32)
+            total[slot] = total[slot] + share
+        return carry
+
+    lax.fori_loop(0, table.shape[0], add, 0, unroll=2)
 
     def divide(at, carry):
-        spot = where(at)
-        patch[spot] = patch[spot] * inverse[at]
-        return carry
-
-    lax.fori_loop(0, SLOT_ROWS * SLOT_COLS, divide, 0, unroll=4)
-
-    def pick(at, carry):
-        picked[at] = patch[where(slot[at])].astype(picked.dtype)
-        return carry
-
-    lax.fori_loop(0, arrived.shape[0], pick, 0, unroll=4)
+        for column in range(SLOT_COLS):
+            number = at * SLOT_COLS + column
+            weights = jnp.maximum(jnp.full((1, BLOCK), total[number], jnp.float32), 1.0)
+            mean = sums[number] * (1.0 / weights)
+            patch[
+                pl.ds(pl.multiple_of(at * BLOCK, BLOCK), BLOCK),
+                column * BLOCK : (column + 1) * BLOCK,
+            ] = mean
+            value[number] = mean.astype(value.dtype)
+        return carry
+
+    lax.fori_loop(0, SLOT_ROWS, divide, 0)
+    value[slots] = blank.astype(value.dtype)
 
 
 def difference_kernel(
@@ -330,9 +385,7 @@
     bases = row_taps.shape[0]
     blocks = (rows // BLOCK) * (cols // BLOCK)
     capacity = max(2, (2 * blocks + devices - 1) // devices)
-    slots = SLOT_ROWS * SLOT_COLS
     buffered = devices * capacity
-    myself = lax.axis_index("exp") * n_tile + lax.axis_index("tile")
     params = pltpu.CompilerParams(vmem_limit_bytes=VMEM_BYTES)
     mine = exposure[0]
 
@@ -341,32 +394,8 @@
     row_bands = row_bands.reshape(bases * BLOCK, BLOCK + 2 * RIM)
     column_bands = banded_transposed(column_taps, 3 * BLOCK, BLOCK, BLOCK - HALF)
 
-    dest_all = route_device.reshape(devices, blocks)
-    slot_all = route_slot.reshape(devices, blocks)
-    weight_all = weight.reshape(devices)
-    earlier = jnp.arange(blocks)[:, None] > jnp.arange(blocks)[None, :]
-    same = dest_all[:, :, None] == dest_all[:, None, :]
-    rank_all = jnp.sum(same & earlier[None], axis=2, dtype=jnp.int32)
-    place_all = dest_all * capacity + rank_all
-    place = lax.dynamic_index_in_dim(place_all, myself, 0, keepdims=False)
-    ident = lax.dynamic_index_in_dim(warp_id.reshape(devices, blocks), myself, 0, keepdims=False)
-    taken = place[None, :] == jnp.arange(buffered, dtype=jnp.int32)[:, None]
-    source = jnp.min(
-        jnp.where(taken, jnp.arange(blocks, dtype=jnp.int32)[None, :], blocks), axis=1
-    )
-    spot_ident = jnp.sum(jnp.where(taken, ident[None, :], 0), axis=1, dtype=jnp.int32)
-    my_weight = lax.dynamic_index_in_dim(weight_all, myself, 0, keepdims=True)
-    hit = (dest_all[:, None, :] == myself) & (
-        rank_all[:, None, :] == jnp.arange(capacity, dtype=jnp.int32)[None, :, None]
-    )
-    slot = jnp.sum(jnp.where(hit, slot_all[:, None, :], 0), axis=2, dtype=jnp.int32)
-    slot = slot.reshape(buffered)
-    valid = jnp.any(hit, axis=2).reshape(buffered).astype(jnp.int32)
-    owned = (slot_all[None] == jnp.arange(slots, dtype=jnp.int32)[:, None, None]) & (
-        dest_all == myself
-    )[None]
-    total = jnp.sum(jnp.where(owned, weight_all[None, :, None], 0.0), axis=(1, 2))
-    inverse = 1.0 / jnp.maximum(total, 1.0)
+    route = route_device.reshape(devices, blocks)
+    slot = route_slot.reshape(devices, blocks)
 
     work = [
         pltpu.VMEM((rows + 2 * RIM, cols), jnp.bfloat16),
@@ -375,44 +404,56 @@
     ]
     semaphores = [pltpu.SemaphoreType.DMA((devices,)), pltpu.SemaphoreType.DMA((devices,))]
     buffer = jax.ShapeDtypeStruct((buffered, BLOCK, BLOCK), jnp.bfloat16)
-    matched = pl.pallas_call(
-        match_kernel,
-        out_shape=jax.ShapeDtypeStruct((blocks + 1, BLOCK, BLOCK), jnp.bfloat16),
-        in_specs=scalars(1) + vectors(5),
-        out_specs=pl.BlockSpec(memory_space=pltpu.VMEM),
-        scratch_shapes=work,
+    matched, place, source, ident = pl.pallas_call(
+        functools.partial(match_kernel, capacity),
+        out_shape=(
+            jax.ShapeDtypeStruct((blocks + 1, BLOCK, BLOCK), jnp.bfloat16),
+            jax.ShapeDtypeStruct((blocks,), jnp.int32),
+            jax.ShapeDtypeStruct((buffered,), jnp.int32),
+            jax.ShapeDtypeStruct((buffered,), jnp.int32),
+        ),
+        in_specs=scalars(3) + vectors(5),
+        out_specs=tuple(vectors(1) + scalars(3)),
+        scratch_shapes=work + [pltpu.SMEM((devices,), jnp.int32)],
         compiler_params=params,
-    )(basis_coef, above, mine, below, row_bands, column_bands)
-    arrived = pl.pallas_call(
+    )(
+        basis_coef, route, warp_id.reshape(devices, blocks), above, mine, below, row_bands,
+        column_bands,
+    )
+    arrived, table = pl.pallas_call(
         functools.partial(send_kernel, n_exp, n_tile),
-        out_shape=buffer,
-        in_specs=scalars(3) + vectors(3),
-        out_specs=pl.BlockSpec(memory_space=pltpu.VMEM),
+        out_shape=(buffer, jax.ShapeDtypeStruct((devices, capacity), jnp.int32)),
+        in_specs=scalars(3) + vectors(5),
+        out_specs=tuple(vectors(2)),
         scratch_shapes=[pltpu.VMEM(buffer.shape, buffer.dtype)] + semaphores,
         compiler_params=pltpu.CompilerParams(
             vmem_limit_bytes=VMEM_BYTES, collective_id=0, has_side_effects=True
         ),
-    )(source, spot_ident, my_weight, matched, warp_rows, warp_columns)
-    patch, picked = pl.pallas_call(
-        coadd_kernel,
+    )(source, ident, weight, matched, warp_rows, warp_columns, route, slot)
+    patch, value = pl.pallas_call(
+        functools.partial(coadd_kernel, n_tile),
         out_shape=(
             jax.ShapeDtypeStruct((SLOT_ROWS * BLOCK, SLOT_COLS * BLOCK), jnp.float32),
-            buffer,
+            jax.ShapeDtypeStruct((SLOT_ROWS * SLOT_COLS + 1, BLOCK, BLOCK), jnp.bfloat16),
         ),
-        in_specs=scalars(3) + vectors(1),
+        in_specs=scalars(2) + vectors(1),
         out_specs=tuple(vectors(2)),
+        scratch_shapes=[
+            pltpu.VMEM((SLOT_ROWS * SLOT_COLS + 1, BLOCK, BLOCK), jnp.float32),
+            pltpu.SMEM((SLOT_ROWS * SLOT_COLS + 1,), jnp.float32),
+        ],
         compiler_params=params,
-    )(slot, valid, inverse, arrived)
+    )(table, weight, arrived)
     template = pl.pallas_call(
         functools.partial(return_kernel, n_exp, n_tile),
         out_shape=jax.ShapeDtypeStruct((rows, cols), jnp.bfloat16),
-        in_specs=scalars(2) + vectors(3),
+        in_specs=scalars(3) + vectors(3),
         out_specs=pl.BlockSpec(memory_space=pltpu.VMEM),
-        scratch_shapes=[pltpu.VMEM(buffer.shape, buffer.dtype)] * 2 + semaphores,
+        scratch_shapes=[pltpu.VMEM(buffer.shape, buffer.dtype)] * 3 + semaphores,
         compiler_params=pltpu.CompilerParams(
             vmem_limit_bytes=VMEM_BYTES, collective_id=1, has_side_effects=True
         ),
-    )(spot_ident, place, picked, warp_rows, warp_columns)
+    )(ident, place, table, value, warp_rows, warp_columns)
     template_above, template_below = halo(template, "tile")
     difference = pl.pallas_call(
         difference_kernel,

time: 289 us -> 265 us (0.917)
  Pallas kernels: 251 us -> 233 us
  other arithmetic: 14.4 us -> 10.7 us
    pallas_call x1, Pallas kernels: 114 us -> 101 us  [shards(): pl.pallas_call(functools.partial(return_kernel, n_exp, n_tile), out_shape...]
    pallas_call x3, Pallas kernels: 124 us -> 119 us  [the longest x1 99.7 us: shards(): pl.pallas_call(functools.partial(send_kernel, n_exp, n_tile), out_shape=(...]
  transfers between devices with their start and end apart: 4 -> 4, of which waited for: 2 -> 2; matrix products, arithmetic and copies ran while one was open for 6% -> 4% of each run, Pallas kernels for 0% -> 0%
where the time goes in v3:
time: 265 us; the launch traced here: 263 us
  Pallas kernels  233 us (88%)
  starting transfers between devices  12.9 us (5%)
  other arithmetic  10.7 us (4%)
  local copies, waits for them, and re-layouts  4.08 us (2%)
    pallas_call x1, Pallas kernels, shards(): pl.pallas_call(functools.partial(return_kernel, n_exp, n_tile), out_shape...  101 us
    pallas_call x1, Pallas kernels, shards(): pl.pallas_call(functools.partial(send_kernel, n_exp, n_tile), out_shape=(...  99.7 us
    pallas_call x1, Pallas kernels, shards(): pl.pallas_call(difference_kernel, out_shape=jax.ShapeDtypeStruct((rows, c...  12.6 us
    pallas_call x1, Pallas kernels, shards(): pl.pallas_call(functools.partial(match_kernel, capacity), out_shape=(jax....  12.3 us
    ppermute x2, starting transfers between devices, halo(): above = lax.ppermute(image[-RIM:], axis, forward)  7.56 us
    pallas_call x1, Pallas kernels, shards(): pl.pallas_call(functools.partial(coadd_kernel, n_tile), out_shape=(jax.Sh...  6.98 us
    ppermute x2, starting transfers between devices, halo(): below = lax.ppermute(image[:RIM], axis, backward)  5.36 us
  transfers between devices with their start and end apart: 4, of which 2 were waited for; matrix products, arithmetic and copies ran while one was open for 4% of the time, Pallas kernels for 0%

profile of v3, /device:TPU:11, one launch (start us, length us, event | category | flops | bytes accessed | tf_op | source)
XLA Modules:
  0.0 263.2 jit_solution(14531442995598012202)
XLA Ops:
  0.6 1.0 slice_bitcast_fusion
  1.6 2.6 collective-permute-start.1
  4.2 3.9 %collective-permute-start = (bf16[16,4096]{1,0:T(8,128)(2,1)S(1)}, bf16[16,4096]{1,0:T(8,128)(2,1)S(1)}, u32[]{:S(2)}, u32[]{:S(2)}) collective-permute-start(bf16[16,4096]{1,0:T(8,128)(2,1)S(1)} %get-tuple-element.63), channel_id=1, source_target_pairs={{0,1},{1,2},{2,3},{3,4},{4,5},{5,6},{6,7},{8,9},{9,10},{10,11},{11... | collective-permute-start | bytes 393224 | tf_op jit(solution)/shard_map/ppermute | solution.py:23
  8.1 1.0 convert_reduce_fusion.22
  9.1 1.9 convert_reduce_fusion.41
  11.0 1.0 convert_reduce_fusion.1
  11.9 1.9 convert_reduce_fusion.20
  14.6 0.1 broadcast_bitcast_fusion.20
  14.7 0.1 broadcast_bitcast_fusion
  14.8 0.1 broadcast_bitcast_fusion.2
  15.4 2.0 add_convert_fusion.column_bands
  17.4 2.3 add_convert_fusion.1.row_bands
  19.7 0.6 copy-done.2
  20.4 12.3 %shard_map.113 = (bf16[65,128,128]{2,1,0:T(8,128)(2,1)}, s32[64]{0:T(128)}, s32[128]{0:T(128)}, s32[128]{0:T(128)}) custom-call(f32[1,3]{1,0:T(1,128)} %coef.3, s32[32,64]{1,0:T(8,128)} %bitcast.96, s32[32,64]{1,0:T(8,128)} %bitcast.98, bf16[16,4096]{1,0:T(8,128)(2,1)} %copy-done.3, bf16[256,4096]{1,0:T(8,128)(2,1)} %bitcast.93, bf16[16,4096]{1,0:T(8,128)(2,1)} %copy-done.2, ...), custom_call_target="tpu_custom_call" | custom-call | tf_op jit(solution)/shard_map/pallas_call | solution.py:407
  32.7 99.7 %shard_map.114 = (bf16[128,128,128]{2,1,0:T(8,128)(2,1)}, s32[32,4]{1,0:T(8,128)}) custom-call(s32[128]{0:T(128)} %get-tuple-element.10.source, s32[128]{0:T(128)} %get-tuple-element.11.ident, f32[4,8]{1,0:T(4,128)} %weight.3, bf16[65,128,128]{2,1,0:T(8,128)(2,1)} %get-tuple-element.12.matched, bf16[64,128,128]{2,1,0:T(8,128)(2,1)} %warp_rows.3, ...), custom_call_target="tpu_custom_call" | custom-call | tf_op jit(solution)/shard_map/pallas_call | solution.py:423
  132.5 7.0 %shard_map.115 = (f32[1024,1024]{1,0:T(8,128)}, bf16[65,128,128]{2,1,0:T(8,128)(2,1)}) custom-call(s32[32,4]{1,0:T(8,128)} %get-tuple-element.13.table, f32[4,8]{1,0:T(4,128)} %weight.3, bf16[128,128,128]{2,1,0:T(8,128)(2,1)} %get-tuple-element.14.arrived), custom_call_target="tpu_custom_call" | custom-call | tf_op jit(solution)/shard_map/pallas_call | solution.py:433
  139.5 101.1 %shard_map.116.image = bf16[256,4096]{1,0:T(8,128)(2,1)} custom-call(s32[128]{0:T(128)} %get-tuple-element.11.ident, s32[64]{0:T(128)} %get-tuple-element.16.place, s32[32,4]{1,0:T(8,128)} %get-tuple-element.13.table, bf16[65,128,128]{2,1,0:T(8,128)(2,1)} %get-tuple-element.17.value, bf16[64,128,128]{2,1,0:T(8,128)(2,1)} %warp_rows.3, ...), custom_call_target="tpu_custom_call" | custom-call | tf_op jit(solution)/shard_map/pallas_call | solution.py:447
  240.6 1.0 fusion.42
  241.6 2.8 %collective-permute-start.3 = (bf16[16,4096]{1,0:T(8,128)(2,1)S(1)}, bf16[16,4096]{1,0:T(8,128)(2,1)S(1)}, u32[]{:S(2)}, u32[]{:S(2)}) collective-permute-start(bf16[16,4096]{1,0:T(8,128)(2,1)S(1)} %get-tuple-element.60), channel_id=1, source_target_pairs={{1,0},{2,1},{3,2},{4,3},{5,4},{6,5},{7,6},{9,8},{10,9},{11,10},{12... | collective-permute-start | bytes 393224 | tf_op jit(solution)/shard_map/ppermute | solution.py:24
  244.4 3.7 %collective-permute-start.2 = (bf16[16,4096]{1,0:T(8,128)(2,1)S(1)}, bf16[16,4096]{1,0:T(8,128)(2,1)S(1)}, u32[]{:S(2)}, u32[]{:S(2)}) collective-permute-start(bf16[16,4096]{1,0:T(8,128)(2,1)S(1)} %get-tuple-element.61), channel_id=1, source_target_pairs={{0,1},{1,2},{2,3},{3,4},{4,5},{5,6},{6,7},{8,9},{9,10},{10,11},{11... | collective-permute-start | bytes 393224 | tf_op jit(solution)/shard_map/ppermute | solution.py:23
  248.1 0.7 collective-permute-done.3.below
  248.8 1.2 collective-permute-done.2.above
  250.0 0.7 copy-done.1
  250.6 12.6 %shard_map.117 = f32[256,4096]{1,0:T(8,128)} custom-call(f32[1,3]{1,0:T(1,128)} %coef.3, bf16[16,4096]{1,0:T(8,128)(2,1)} %copy-done.1, bf16[256,4096]{1,0:T(8,128)(2,1)} %shard_map.116.image, bf16[16,4096]{1,0:T(8,128)(2,1)} %copy-done, bf16[384,160]{1,0:T(8,128)(2,1)} %add_convert_fusion.1.row_bands, bf16[3,384,128]{2,1,0:T(8,128)(2,1)} %add_convert_fusion.column_bands, ...), custom_call_target="tpu_custom_call" | custom-call | tf_op jit(solution)/shard_map/pallas_call | solution.py:458
  (38 shorter events, 1.3 us)
Async XLA Ops:
  1.6 18.1 %collective-permute-start.1 = (bf16[16,4096]{1,0:T(8,128)(2,1)S(1)}, bf16[16,4096]{1,0:T(8,128)(2,1)S(1)}, u32[]{:S(2)}, u32[]{:S(2)}) collective-permute-start(bf16[16,4096]{1,0:T(8,128)(2,1)S(1)} %get-tuple-element.62), channel_id=1, source_target_pairs={{1,0},{2,1},{3,2},{4,3},{5,4},{6,5},{7,6},{9,8},{10,9},{11,10},{12... | collective-permute-start | bytes 393224 | tf_op jit(solution)/shard_map/ppermute | solution.py:24
  4.2 15.5 %collective-permute-start = (bf16[16,4096]{1,0:T(8,128)(2,1)S(1)}, bf16[16,4096]{1,0:T(8,128)(2,1)S(1)}, u32[]{:S(2)}, u32[]{:S(2)}) collective-permute-start(bf16[16,4096]{1,0:T(8,128)(2,1)S(1)} %get-tuple-element.63), channel_id=1, source_target_pairs={{0,1},{1,2},{2,3},{3,4},{4,5},{5,6},{6,7},{8,9},{9,10},{10,11},{11... | collective-permute-start | bytes 393224 | tf_op jit(solution)/shard_map/ppermute | solution.py:23
  19.7 0.6 copy-start.2
  19.7 0.7 copy-start.3
  241.6 7.2 %collective-permute-start.3 = (bf16[16,4096]{1,0:T(8,128)(2,1)S(1)}, bf16[16,4096]{1,0:T(8,128)(2,1)S(1)}, u32[]{:S(2)}, u32[]{:S(2)}) collective-permute-start(bf16[16,4096]{1,0:T(8,128)(2,1)S(1)} %get-tuple-element.60), channel_id=1, source_target_pairs={{1,0},{2,1},{3,2},{4,3},{5,4},{6,5},{7,6},{9,8},{10,9},{11,10},{12... | collective-permute-start | bytes 393224 | tf_op jit(solution)/shard_map/ppermute | solution.py:24
  244.4 5.6 %collective-permute-start.2 = (bf16[16,4096]{1,0:T(8,128)(2,1)S(1)}, bf16[16,4096]{1,0:T(8,128)(2,1)S(1)}, u32[]{:S(2)}, u32[]{:S(2)}) collective-permute-start(bf16[16,4096]{1,0:T(8,128)(2,1)S(1)} %get-tuple-element.61), channel_id=1, source_target_pairs={{0,1},{1,2},{2,3},{3,4},{4,5},{5,6},{6,7},{8,9},{9,10},{10,11},{11... | collective-permute-start | bytes 393224 | tf_op jit(solution)/shard_map/ppermute | solution.py:23
  248.8 1.2 copy-start
  250.0 0.7 copy-start.1

commit v4 on v3

--- a/solution.py
+++ b/solution.py
@@ -13,43 +13,156 @@
 WIDE = 2 * BLOCK
 SLOT_ROWS = 8
 SLOT_COLS = 8
-VMEM_BYTES = 56 * 1024 * 1024
-
-
-def halo(image, axis):
-    count = lax.axis_size(axis)
-    forward = [(i, i + 1) for i in range(count - 1)]
-    backward = [(target, source) for source, target in forward]
-    above = lax.ppermute(image[-RIM:], axis, forward)
-    below = lax.ppermute(image[:RIM], axis, backward)
-    return above, below
-
-
-def banded(taps, rows, cols, offset):
-    shape = (rows, cols)
+
+
+def edge_copies(image, above, below, send_sem, recv_sem):
+    rows = image.shape[0]
+    row, tile, count = lax.axis_index("exp"), lax.axis_index("tile"), lax.axis_size("tile")
+    onward = pltpu.make_async_remote_copy(
+        src_ref=image.at[pl.ds(rows - RIM, RIM)],
+        dst_ref=above,
+        send_sem=send_sem.at[0],
+        recv_sem=recv_sem.at[0],
+        device_id=(row, lax.rem(tile + 1, count)),
+        device_id_type=pl.DeviceIdType.MESH,
+    )
+    backward = pltpu.make_async_remote_copy(
+        src_ref=image.at[pl.ds(0, RIM)],
+        dst_ref=below,
+        send_sem=send_sem.at[1],
+        recv_sem=recv_sem.at[1],
+        device_id=(row, lax.rem(tile + count - 1, count)),
+        device_id_type=pl.DeviceIdType.MESH,
+    )
+    return onward, backward
+
+
+def start_edges(image, above, below, send_sem, recv_sem):
+    tile, count = lax.axis_index("tile"), lax.axis_size("tile")
+    onward, backward = edge_copies(image, above, below, send_sem, recv_sem)
+
+    @pl.when(tile < count - 1)
+    def _():
+        onward.start()
+
+    @pl.when(tile > 0)
+    def _():
+        backward.start()
+
+    @pl.when(tile == 0)
+    def _():
+        above[...] = jnp.zeros_like(above)
+
+    @pl.when(tile == count - 1)
+    def _():
+        below[...] = jnp.zeros_like(below)
+
+
+def finish_edges(image, above, below, send_sem, recv_sem):
+    tile, count = lax.axis_index("tile"), lax.axis_size("tile")
+    onward, backward = edge_copies(image, above, below, send_sem, recv_sem)
+
+    @pl.when(tile < count - 1)
+    def _():
+        onward.wait_send()
+        backward.wait_recv()
+
+    @pl.when(tile > 0)
+    def _():
+        backward.wait_send()
+        onward.wait_recv()
+
+
+def banded(taps, basis, lag):
+    total = jnp.zeros(lag.shape, jnp.float32)
+    for tap in range(taps.shape[1]):
+        value = jnp.broadcast_to(taps[basis : basis + 1, tap : tap + 1], lag.shape)
+        total = jnp.where(lag == tap, value, total)
+    return total.astype(jnp.bfloat16)
+
+
+def ranked(hit):
+    count = hit.shape[1]
+    later = (
+        lax.broadcasted_iota(jnp.int32, (count, count), 0)
+        < lax.broadcasted_iota(jnp.int32, (count, count), 1)
+    )
+    ranks = jnp.dot(
+        hit.astype(jnp.float32), later.astype(jnp.float32), preferred_element_type=jnp.float32
+    )
+    return ranks.astype(jnp.int32)
+
+
+def by_rank(hit, ranks, values, none, shape):
+    column = lax.broadcasted_iota(jnp.int32, shape, 1)
+    filled = jnp.zeros(shape, jnp.int32)
+    for rank in range(shape[1]):
+        chosen = jnp.where(hit & (ranks == rank), values - none, 0)
+        filled = jnp.where(column == rank, jnp.sum(chosen, axis=1, keepdims=True) + none, filled)
+    return filled
+
+
+def prepare_kernel(
+    image, row_taps, column_taps, route, warp_id, above, below, row_bands, bands, source, ident,
+    place, send_sem, recv_sem,
+):
+    row, tile, count = lax.axis_index("exp"), lax.axis_index("tile"), lax.axis_size("tile")
+    me = row * count + tile
+    barrier = pltpu.get_barrier_semaphore()
+
+    @pl.when(tile < count - 1)
+    def _():
+        pl.semaphore_signal(
+            barrier, inc=1, device_id=(row, lax.rem(tile + 1, count)),
+            device_id_type=pl.DeviceIdType.MESH,
+        )
+
+    @pl.when(tile > 0)
+    def _():
+        pl.semaphore_signal(
+            barrier, inc=1, device_id=(row, lax.rem(tile + count - 1, count)),
+            device_id_type=pl.DeviceIdType.MESH,
+        )
+
+    bases = row_taps.shape[0]
+    taps = row_taps[...].astype(jnp.float32)
+    shape = (BLOCK, BLOCK + 2 * RIM)
     lag = lax.broadcasted_iota(jnp.int32, shape, 1) - lax.broadcasted_iota(jnp.int32, shape, 0)
-    lag = lag - offset
-    count = taps.shape[1]
-    total = jnp.zeros((taps.shape[0], rows, cols), jnp.float32)
-    for tap in range(count):
-        value = taps[:, tap, None, None].astype(jnp.float32)
-        total = total + jnp.where(lag == tap, value, 0.0)
-    return total.astype(jnp.bfloat16)
-
-
-def banded_transposed(taps, rows, cols, offset):
-    shape = (rows, cols)
+    for basis in range(bases):
+        row_bands[basis * BLOCK : (basis + 1) * BLOCK, :] = banded(
+            taps, basis, lag - (RIM - HALF)
+        )
+
+    peers = jnp.minimum(tile, 1) + jnp.minimum(count - 1 - tile, 1)
+    pl.semaphore_wait(barrier, peers)
+
+    start_edges(image, above, below, send_sem, recv_sem)
+
+    taps = column_taps[...].astype(jnp.float32)
+    shape = (3 * BLOCK, BLOCK)
     lag = lax.broadcasted_iota(jnp.int32, shape, 0) - lax.broadcasted_iota(jnp.int32, shape, 1)
-    lag = lag - offset
-    count = taps.shape[1]
-    total = jnp.zeros((taps.shape[0], rows, cols), jnp.float32)
-    for tap in range(count):
-        value = taps[:, tap, None, None].astype(jnp.float32)
-        total = total + jnp.where(lag == tap, value, 0.0)
-    return total.astype(jnp.bfloat16)
-
-
-def row_stage(coef, above, image, below, row_bands, column_bands, padded, passes, bands):
+    bands[...] = jnp.zeros_like(bands)
+    for basis in range(bases):
+        band = banded(taps, basis, lag - (BLOCK - HALF))
+        for side in range(WIDE // BLOCK):
+            top = side * BLOCK
+            bands[basis, top : top + 3 * BLOCK, top : top + BLOCK] = band
+
+    devices, blocks = route.shape
+    capacity = source.shape[1]
+    device = lax.broadcasted_iota(jnp.int32, (devices, blocks), 0)
+    hit = jnp.broadcast_to(route[pl.ds(me, 1), :], (devices, blocks)) == device
+    ranks = ranked(hit)
+    number = lax.broadcasted_iota(jnp.int32, (devices, blocks), 1)
+    source[...] = by_rank(hit, ranks, number, blocks, source.shape)
+    mine = jnp.broadcast_to(warp_id[pl.ds(me, 1), :], (devices, blocks))
+    ident[...] = by_rank(hit, ranks, mine, 0, ident.shape)
+    place[...] = jnp.sum(jnp.where(hit, device * capacity + ranks, 0), axis=0, keepdims=True)
+
+    finish_edges(image, above, below, send_sem, recv_sem)
+
+
+def row_stage(coef, above, image, below, row_bands, padded, passes):
     bases = passes.shape[0]
     rows, cols = image.shape
     blocks = rows // BLOCK
@@ -58,10 +171,6 @@
     padded[RIM : RIM + rows, :] = image[...]
     padded[RIM + rows :, :] = below[...]
     edge = jnp.zeros((rows, BLOCK), passes.dtype)
-    bands[...] = jnp.zeros_like(bands)
-    for side in range(WIDE // BLOCK):
-        top = side * BLOCK
-        bands[:, top : top + 3 * BLOCK, top : top + BLOCK] = column_bands[...]
     for basis in range(bases):
         passes[basis, :, :BLOCK] = edge
         passes[basis, :, BLOCK + cols :] = edge
@@ -97,36 +206,11 @@
     return total
 
 
-def match_kernel(
-    capacity, coef, route, warp_id, above, image, below, row_bands, column_bands, matched, place,
-    source, ident, padded, passes, bands, count,
-):
+def match_kernel(coef, above, image, below, row_bands, bands, matched, padded, passes):
     rows, cols = image.shape
-    me = lax.axis_index("exp") * lax.axis_size("tile") + lax.axis_index("tile")
-
-    def clear(at, carry):
-        count[at] = 0
-        for rank in range(capacity):
-            source[at * capacity + rank] = route.shape[1]
-            ident[at * capacity + rank] = 0
-        return carry
-
-    lax.fori_loop(0, route.shape[0], clear, 0)
-
-    def assign(at, carry):
-        device = route[me, at]
-        rank = count[device]
-        count[device] = rank + 1
-        spot = device * capacity + rank
-        place[at] = spot
-        source[spot] = at
-        ident[spot] = warp_id[me, at]
-        return carry
-
-    lax.fori_loop(0, route.shape[1], assign, 0)
     blocks = rows // BLOCK
     across = cols // BLOCK
-    row_stage(coef, above, image, below, row_bands, column_bands, padded, passes, bands)
+    row_stage(coef, above, image, below, row_bands, padded, passes)
     matched[blocks * across] = jnp.zeros((BLOCK, BLOCK), matched.dtype)
 
     def step(at, carry):
@@ -207,9 +291,9 @@
     def warp(other, target):
         for rank in range(capacity):
             spot = other * capacity + rank
-            which = ident[spot]
+            which = ident[other, rank]
             first = jnp.dot(
-                warp_rows[which], matched[source[spot]], preferred_element_type=jnp.float32
+                warp_rows[which], matched[source[other, rank]], preferred_element_type=jnp.float32
             ).astype(jnp.bfloat16)
             second = lax.dot_general(
                 first,
@@ -228,23 +312,8 @@
     lax.fori_loop(0, devices - 1, step, 0)
     warp(me, arrived)
 
-    count = route.shape[1]
     hit = route[...] == me
-    later = (
-        lax.broadcasted_iota(jnp.int32, (count, count), 0)
-        < lax.broadcasted_iota(jnp.int32, (count, count), 1)
-    )
-    rank_of = jnp.dot(
-        hit.astype(jnp.float32), later.astype(jnp.float32), preferred_element_type=jnp.float32
-    ).astype(jnp.int32)
-    column = lax.broadcasted_iota(jnp.int32, table.shape, 1)
-    filled = jnp.zeros(table.shape, jnp.int32)
-    none = SLOT_ROWS * SLOT_COLS
-    for rank in range(capacity):
-        chosen = jnp.where(hit & (rank_of == rank), slot[...] - none, 0)
-        found = jnp.sum(chosen, axis=1, keepdims=True) + none
-        filled = jnp.where(column == rank, found, filled)
-    table[...] = filled
+    table[...] = by_rank(hit, ranked(hit), slot[...], SLOT_ROWS * SLOT_COLS, table.shape)
 
     def finish(at, carry):
         _, other = partner(me, at, devices)
@@ -255,8 +324,8 @@
 
 
 def return_kernel(
-    n_exp, n_tile, ident, place, table, value, warp_rows, warp_columns, image, picked, returned,
-    unwarped, send_sem, recv_sem,
+    n_exp, n_tile, ident, place, table, value, warp_rows, warp_columns, image, above, below,
+    picked, returned, unwarped, send_sem, recv_sem, edge_send, edge_recv,
 ):
     devices = n_exp * n_tile
     capacity = picked.shape[0] // devices
@@ -279,7 +348,7 @@
     def unwarp(other, origin):
         for rank in range(capacity):
             spot = other * capacity + rank
-            which = ident[spot]
+            which = ident[other, rank]
             back = lax.dot_general(
                 warp_rows[which],
                 origin[spot],
@@ -304,11 +373,13 @@
         left = pl.multiple_of(at * BLOCK, BLOCK)
         for block in range(image.shape[0] // BLOCK):
             image[block * BLOCK : (block + 1) * BLOCK, pl.ds(left, BLOCK)] = unwarped[
-                place[block * across + at]
+                place[0, block * across + at]
             ]
         return carry
 
     lax.fori_loop(0, across, gather, 0)
+    start_edges(image, above, below, edge_send, edge_recv)
+    finish_edges(image, above, below, edge_send, edge_recv)
 
 
 def coadd_kernel(n_tile, table, weight, arrived, patch, value, sums, total):
@@ -350,11 +421,10 @@
 
 
 def difference_kernel(
-    coef, above, image, below, row_bands, column_bands, exposure, difference, padded, passes,
-    bands,
+    coef, above, image, below, row_bands, bands, exposure, difference, padded, passes
 ):
     cols = image.shape[1]
-    row_stage(coef, above, image, below, row_bands, column_bands, padded, passes, bands)
+    row_stage(coef, above, image, below, row_bands, padded, passes)
 
     def step(at, carry):
         start = pl.multiple_of(at * WIDE, WIDE)
@@ -385,86 +455,97 @@
     bases = row_taps.shape[0]
     blocks = (rows // BLOCK) * (cols // BLOCK)
     capacity = max(2, (2 * blocks + devices - 1) // devices)
+    slots = SLOT_ROWS * SLOT_COLS
     buffered = devices * capacity
-    params = pltpu.CompilerParams(vmem_limit_bytes=VMEM_BYTES)
     mine = exposure[0]
-
-    above, below = halo(mine, "tile")
-    row_bands = banded(row_taps, BLOCK, BLOCK + 2 * RIM, RIM - HALF)
-    row_bands = row_bands.reshape(bases * BLOCK, BLOCK + 2 * RIM)
-    column_bands = banded_transposed(column_taps, 3 * BLOCK, BLOCK, BLOCK - HALF)
-
     route = route_device.reshape(devices, blocks)
     slot = route_slot.reshape(devices, blocks)
 
+    def shape(*dims, dtype=jnp.bfloat16):
+        return jax.ShapeDtypeStruct(dims, dtype)
+
+    def params(units, **more):
+        return pltpu.CompilerParams(vmem_limit_bytes=units * 1024 * 1024, **more)
+
+    buffer = shape(buffered, BLOCK, BLOCK)
+    buffer_units = (2 * buffered * BLOCK * BLOCK) // (1024 * 1024)
+    bank_units = (4 * warp_rows.size) // (1024 * 1024)
+    image_units = (2 * rows * cols) // (1024 * 1024)
+    work_units = (bases + 2) * image_units
+    slot_units = (4 * slots * BLOCK * BLOCK) // (1024 * 1024)
+    spare = 6
+    tables = shape(devices, capacity, dtype=jnp.int32)
+    edge = shape(RIM, cols)
+    pair = [pltpu.SemaphoreType.DMA((2,)), pltpu.SemaphoreType.DMA((2,))]
+    semaphores = [pltpu.SemaphoreType.DMA((devices,)), pltpu.SemaphoreType.DMA((devices,))]
     work = [
         pltpu.VMEM((rows + 2 * RIM, cols), jnp.bfloat16),
         pltpu.VMEM((bases, rows, cols + 2 * BLOCK), jnp.bfloat16),
-        pltpu.VMEM((bases, 2 * WIDE, WIDE), jnp.bfloat16),
     ]
-    semaphores = [pltpu.SemaphoreType.DMA((devices,)), pltpu.SemaphoreType.DMA((devices,))]
-    buffer = jax.ShapeDtypeStruct((buffered, BLOCK, BLOCK), jnp.bfloat16)
-    matched, place, source, ident = pl.pallas_call(
-        functools.partial(match_kernel, capacity),
+
+    above, below, row_bands, bands, source, ident, place = pl.pallas_call(
+        prepare_kernel,
         out_shape=(
-            jax.ShapeDtypeStruct((blocks + 1, BLOCK, BLOCK), jnp.bfloat16),
-            jax.ShapeDtypeStruct((blocks,), jnp.int32),
-            jax.ShapeDtypeStruct((buffered,), jnp.int32),
-            jax.ShapeDtypeStruct((buffered,), jnp.int32),
+            edge, edge, shape(bases * BLOCK, BLOCK + 2 * RIM), shape(bases, 2 * WIDE, WIDE),
+            tables, tables, shape(1, blocks, dtype=jnp.int32),
         ),
-        in_specs=scalars(3) + vectors(5),
-        out_specs=tuple(vectors(1) + scalars(3)),
-        scratch_shapes=work + [pltpu.SMEM((devices,), jnp.int32)],
-        compiler_params=params,
-    )(
-        basis_coef, route, warp_id.reshape(devices, blocks), above, mine, below, row_bands,
-        column_bands,
-    )
+        in_specs=[pl.BlockSpec(memory_space=pl.ANY)] + vectors(4),
+        out_specs=tuple(vectors(7)),
+        scratch_shapes=pair,
+        compiler_params=params(spare + 4, collective_id=2, has_side_effects=True),
+    )(mine, row_taps, column_taps, route, warp_id.reshape(devices, blocks))
+    matched = pl.pallas_call(
+        match_kernel,
+        out_shape=shape(blocks + 1, BLOCK, BLOCK),
+        in_specs=scalars(1) + vectors(5),
+        out_specs=pl.BlockSpec(memory_space=pltpu.VMEM),
+        scratch_shapes=work,
+        compiler_params=params(work_units + 2 * image_units + spare),
+    )(basis_coef, above, mine, below, row_bands, bands)
     arrived, table = pl.pallas_call(
         functools.partial(send_kernel, n_exp, n_tile),
-        out_shape=(buffer, jax.ShapeDtypeStruct((devices, capacity), jnp.int32)),
+        out_shape=(buffer, tables),
         in_specs=scalars(3) + vectors(5),
         out_specs=tuple(vectors(2)),
         scratch_shapes=[pltpu.VMEM(buffer.shape, buffer.dtype)] + semaphores,
-        compiler_params=pltpu.CompilerParams(
-            vmem_limit_bytes=VMEM_BYTES, collective_id=0, has_side_effects=True
+        compiler_params=params(
+            2 * buffer_units + bank_units + image_units + spare, collective_id=0,
+            has_side_effects=True,
         ),
     )(source, ident, weight, matched, warp_rows, warp_columns, route, slot)
     patch, value = pl.pallas_call(
         functools.partial(coadd_kernel, n_tile),
         out_shape=(
-            jax.ShapeDtypeStruct((SLOT_ROWS * BLOCK, SLOT_COLS * BLOCK), jnp.float32),
-            jax.ShapeDtypeStruct((SLOT_ROWS * SLOT_COLS + 1, BLOCK, BLOCK), jnp.bfloat16),
+            shape(SLOT_ROWS * BLOCK, SLOT_COLS * BLOCK, dtype=jnp.float32),
+            shape(slots + 1, BLOCK, BLOCK),
         ),
         in_specs=scalars(2) + vectors(1),
         out_specs=tuple(vectors(2)),
         scratch_shapes=[
-            pltpu.VMEM((SLOT_ROWS * SLOT_COLS + 1, BLOCK, BLOCK), jnp.float32),
-            pltpu.SMEM((SLOT_ROWS * SLOT_COLS + 1,), jnp.float32),
+            pltpu.VMEM((slots + 1, BLOCK, BLOCK), jnp.float32),
+            pltpu.SMEM((slots + 1,), jnp.float32),
         ],
-        compiler_params=params,
+        compiler_params=params(buffer_units + 3 * slot_units + spare),
     )(table, weight, arrived)
-    template = pl.pallas_call(
+    template, template_above, template_below = pl.pallas_call(
         functools.partial(return_kernel, n_exp, n_tile),
-        out_shape=jax.ShapeDtypeStruct((rows, cols), jnp.bfloat16),
+        out_shape=(shape(rows, cols), edge, edge),
         in_specs=scalars(3) + vectors(3),
-        out_specs=pl.BlockSpec(memory_space=pltpu.VMEM),
-        scratch_shapes=[pltpu.VMEM(buffer.shape, buffer.dtype)] * 3 + semaphores,
-        compiler_params=pltpu.CompilerParams(
-            vmem_limit_bytes=VMEM_BYTES, collective_id=1, has_side_effects=True
+        out_specs=tuple(vectors(3)),
+        scratch_shapes=[pltpu.VMEM(buffer.shape, buffer.dtype)] * 3 + semaphores + pair,
+        compiler_params=params(
+            3 * buffer_units + bank_units + slot_units + image_units + spare, collective_id=1,
+            has_side_effects=True,
         ),
     )(ident, place, table, value, warp_rows, warp_columns)
-    template_above, template_below = halo(template, "tile")
     difference = pl.pallas_call(
         difference_kernel,
-        out_shape=jax.ShapeDtypeStruct((rows, cols), jnp.float32),
+        out_shape=shape(rows, cols, dtype=jnp.float32),
         in_specs=scalars(1) + vectors(6),
         out_specs=pl.BlockSpec(memory_space=pltpu.VMEM),
         scratch_shapes=work,
-        compiler_params=params,
-    )(
-        basis_coef, template_above, template, template_below, row_bands, column_bands, mine
-    )
+        compiler_params=params(work_units + 4 * image_units + spare),
+    )(basis_coef, template_above, template, template_below, row_bands, bands, mine)
     return patch, difference[None]
 
 

time: 265 us -> 236 us (0.89)
  starting transfers between devices: 12.9 us -> 0 us
  other arithmetic: 10.7 us -> 0 us
  Pallas kernels: 233 us -> 230 us
    ppermute x4 -> x0, starting transfers between devices: 12.9 us -> none  [the longest x2 7.56 us: halo(): above = lax.ppermute(image[-RIM:], axis, forward)]
    convert_element_type x6 -> x0, other arithmetic: 9.94 us -> none  [the longest x2 2.87 us: banded_transposed(): value = taps[:, tap, None, None].astype(jnp.float32)]
    unnamed x8 -> x24, local copies, waits for them, and re-layouts: 1.34 us -> 4.42 us
    pallas_call x3 -> x4, Pallas kernels: 31.9 us -> 30.4 us  [the longest x1 10.5 us: shards(): pl.pallas_call(difference_kernel, out_shape=shape(rows, cols, dtype=jnp.f...]
  transfers between devices with their start and end apart: 4 -> 0, of which waited for: 2 -> 0; matrix products, arithmetic and copies ran while one was open for 4% -> 0% of each run, Pallas kernels for 0% -> 0%
where the time goes in v4:
time: 236 us
  Pallas kernels  230 us (97%)
  local copies, waits for them, and re-layouts  4.42 us (2%)
    pallas_call x1, Pallas kernels, shards(): pl.pallas_call(functools.partial(return_kernel, n_exp, n_tile), out_shape...  103 us
    pallas_call x1, Pallas kernels, shards(): pl.pallas_call(functools.partial(send_kernel, n_exp, n_tile), out_shape=(...  97.1 us
    pallas_call x1, Pallas kernels, shards(): pl.pallas_call(difference_kernel, out_shape=shape(rows, cols, dtype=jnp.f...  10.5 us
    pallas_call x1, Pallas kernels, shards(): pl.pallas_call(match_kernel, out_shape=shape(blocks + 1, BLOCK, BLOCK), i...  8.3 us
    pallas_call x1, Pallas kernels, shards(): pl.pallas_call(prepare_kernel, out_shape=(edge, edge, shape(bases * BLOCK...  6.69 us
    pallas_call x1, Pallas kernels, shards(): pl.pallas_call(functools.partial(coadd_kernel, n_tile), out_shape=(shape(...  4.91 us

profile of v4, /device:TPU:11, one launch (start us, length us, event | category | flops | bytes accessed | tf_op | source)
XLA Modules:
  0.0 235.6 jit_solution(10781765904791732319)
XLA Ops:
  0.6 0.0 copy-start.9
  0.6 0.0 copy-start
  0.7 1.6 copy-done
  2.2 0.7 copy-done.4
  3.0 0.7 copy-done.6
  3.7 0.7 copy-done.10
  4.4 0.7 copy-done.11
  5.0 6.7 %shard_map.113 = (bf16[16,4096]{1,0:T(8,128)(2,1)S(1)}, bf16[16,4096]{1,0:T(8,128)(2,1)S(1)}, bf16[384,160]{1,0:T(8,128)(2,1)S(1)}, bf16[3,512,256]{2,1,0:T(8,12...) custom-call(bf16[256,4096]{1,0:T(8,128)(2,1)S(1)} %bitcast.5, ...), custom_call_target="tpu_custom_call" | custom-call | tf_op jit(solution)/shard_map/pallas_call | solution.py:486
  11.7 0.0 copy-done.9
  11.8 0.0 copy-start.2
  11.8 0.0 copy-start.3
  11.8 0.0 copy-start.5
  11.8 0.0 copy-start.7
  11.8 0.0 copy-start.8
  11.8 8.3 %shard_map.114.matched = bf16[65,128,128]{2,1,0:T(8,128)(2,1)S(1)} custom-call(f32[1,3]{1,0:T(1,128)S(1)} %copy-done.9, bf16[16,4096]{1,0:T(8,128)(2,1)S(1)} %get-tuple-element.18.above, bf16[256,4096]{1,0:T(8,128)(2,1)S(1)} %bitcast.6, bf16[16,4096]{1,0:T(8,128)(2,1)S(1)} %get-tuple-element.19.below, bf16[384,160]{1,0:T(8,128)(2,1)S(1)} %get-tuple-element.20.row_bands, ...), custom_call_target="tpu_custom_call" | custom-call | tf_op jit(solution)/shard_map/pallas_call | solution.py:497
  20.1 0.0 copy-done.2
  20.1 0.0 copy-done.3
  20.1 0.0 copy-done.5
  20.1 0.0 copy-done.7
  20.2 0.0 copy-done.8
  20.2 97.1 %shard_map.115 = (bf16[128,128,128]{2,1,0:T(8,128)(2,1)S(1)}, s32[32,4]{1,0:T(8,128)S(1)}) custom-call(s32[32,4]{1,0:T(8,128)S(1)} %get-tuple-element.16.source, s32[32,4]{1,0:T(8,128)S(1)} %get-tuple-element.17.ident, f32[4,8]{1,0:T(4,128)S(1)} %copy-done.8, bf16[65,128,128]{2,1,0:T(8,128)(2,1)S(1)} %shard_map.114.matched, ...), custom_call_target="tpu_custom_call" | custom-call | tf_op jit(solution)/shard_map/pallas_call | solution.py:505
  117.3 4.9 %shard_map.116 = (f32[1024,1024]{1,0:T(8,128)}, bf16[65,128,128]{2,1,0:T(8,128)(2,1)S(1)}) custom-call(s32[32,4]{1,0:T(8,128)S(1)} %get-tuple-element.22.table, f32[4,8]{1,0:T(4,128)S(1)} %copy-done.8, bf16[128,128,128]{2,1,0:T(8,128)(2,1)S(1)} %get-tuple-element.23.arrived), custom_call_target="tpu_custom_call" | custom-call | tf_op jit(solution)/shard_map/pallas_call | solution.py:516
  122.2 102.8 %shard_map.117 = (bf16[256,4096]{1,0:T(8,128)(2,1)S(1)}, bf16[16,4096]{1,0:T(8,128)(2,1)S(1)}, bf16[16,4096]{1,0:T(8,128)(2,1)S(1)}) custom-call(s32[32,4]{1,0:T(8,128)S(1)} %get-tuple-element.17.ident, s32[1,64]{1,0:T(1,128)S(1)} %get-tuple-element.25.place, s32[32,4]{1,0:T(8,128)S(1)} %get-tuple-element.22.table, ...), custom_call_target="tpu_custom_call" | custom-call | tf_op jit(solution)/shard_map/pallas_call | solution.py:530
  225.0 10.5 %shard_map.118 = f32[256,4096]{1,0:T(8,128)} custom-call(f32[1,3]{1,0:T(1,128)S(1)} %copy-done.9, bf16[16,4096]{1,0:T(8,128)(2,1)S(1)} %get-tuple-element.27.above, bf16[256,4096]{1,0:T(8,128)(2,1)S(1)} %get-tuple-element.28.image, bf16[16,4096]{1,0:T(8,128)(2,1)S(1)} %get-tuple-element.29.below, bf16[384,160]{1,0:T(8,128)(2,1)S(1)} %get-tuple-element.20.row_bands, ...), custom_call_target="tpu_custom_call" | custom-call | tf_op jit(solution)/shard_map/pallas_call | solution.py:541
  (6 shorter events, 0.0 us)
Async XLA Ops:
  0.6 11.1 %copy-start.9 = (f32[1,3]{1,0:T(1,128)S(1)}, f32[1,3]{1,0:T(1,128)}, u32[]{:S(2)}) copy-start(f32[1,3]{1,0:T(1,128)} %coef.3) | copy-start | bytes 40
  0.6 1.6 copy-start
  2.2 0.7 copy-start.4
  3.0 0.7 copy-start.6
  3.7 0.7 copy-start.10
  4.4 0.7 copy-start.11
  5.0 6.7 %copy-start.1 = (bf16[1,256,4096]{2,1,0:T(8,128)(2,1)S(1)}, bf16[1,256,4096]{2,1,0:T(8,128)(2,1)}, u32[]{:S(2)}) copy-start(bf16[1,256,4096]{2,1,0:T(8,128)(2,1)} %param.10) | copy-start | bytes 6291460
  11.8 8.4 %copy-start.2 = (bf16[64,128,128]{2,1,0:T(8,128)(2,1)S(1)}, bf16[64,128,128]{2,1,0:T(8,128)(2,1)}, u32[]{:S(2)}) copy-start(bf16[64,128,128]{2,1,0:T(8,128)(2,1)} %warp_rows.3) | copy-start | bytes 6291460
  11.8 8.4 %copy-start.3 = (bf16[64,128,128]{2,1,0:T(8,128)(2,1)S(1)}, bf16[64,128,128]{2,1,0:T(8,128)(2,1)}, u32[]{:S(2)}) copy-start(bf16[64,128,128]{2,1,0:T(8,128)(2,1)} %warp_columns.3) | copy-start | bytes 6291460
  11.8 8.4 %copy-start.5 = (s32[4,8,64]{2,1,0:T(8,128)S(1)}, s32[4,8,64]{2,1,0:T(8,128)}, u32[]{:S(2)}) copy-start(s32[4,8,64]{2,1,0:T(8,128)} %param.17) | copy-start | bytes 24580
  11.8 8.4 %copy-start.7 = (s32[4,8,64]{2,1,0:T(8,128)S(1)}, s32[4,8,64]{2,1,0:T(8,128)}, u32[]{:S(2)}) copy-start(s32[4,8,64]{2,1,0:T(8,128)} %param.18) | copy-start | bytes 24580
  11.8 8.4 %copy-start.8 = (f32[4,8]{1,0:T(4,128)S(1)}, f32[4,8]{1,0:T(4,128)}, u32[]{:S(2)}) copy-start(f32[4,8]{1,0:T(4,128)} %weight.3) | copy-start | bytes 388

commit v5 on v4

--- a/solution.py
+++ b/solution.py
@@ -103,11 +103,15 @@
 
 
 def prepare_kernel(
-    image, row_taps, column_taps, route, warp_id, above, below, row_bands, bands, source, ident,
-    place, send_sem, recv_sem,
+    image, row_taps, column_taps, route_all, warp_all, above, below, row_bands, bands, source,
+    ident, place, send_sem, recv_sem, route, warp_id, load_sem,
 ):
     row, tile, count = lax.axis_index("exp"), lax.axis_index("tile"), lax.axis_size("tile")
     me = row * count + tile
+    load_route = pltpu.make_async_copy(route_all, route, load_sem.at[0])
+    load_warp = pltpu.make_async_copy(warp_all, warp_id, load_sem.at[1])
+    load_route.start()
+    load_warp.start()
     barrier = pltpu.get_barrier_semaphore()
 
     @pl.when(tile < count - 1)
@@ -148,6 +152,8 @@
             top = side * BLOCK
             bands[basis, top : top + 3 * BLOCK, top : top + BLOCK] = band
 
+    load_route.wait()
+    load_warp.wait()
     devices, blocks = route.shape
     capacity = source.shape[1]
     device = lax.broadcasted_iota(jnp.int32, (devices, blocks), 0)
@@ -253,18 +259,19 @@
         return carry
 
     lax.fori_loop(0, devices - 1, hello, 0)
-    pl.semaphore_wait(barrier, devices - 1)
+    return barrier
 
 
 def transfer(source, target, me, other, capacity, n_tile, send_sem, recv_sem):
-    return pltpu.make_async_remote_copy(
-        src_ref=source.at[pl.ds(other * capacity, capacity)],
-        dst_ref=target.at[pl.ds(me * capacity, capacity)],
-        send_sem=send_sem.at[other],
-        recv_sem=recv_sem.at[me],
-        device_id=address(other, n_tile),
-        device_id_type=pl.DeviceIdType.MESH,
-    )
+    for rank in range(capacity):
+        pltpu.make_async_remote_copy(
+            src_ref=source.at[pl.ds(other * capacity + rank, 1)],
+            dst_ref=target.at[pl.ds(me * capacity + rank, 1)],
+            send_sem=send_sem.at[other],
+            recv_sem=recv_sem.at[me],
+            device_id=address(other, n_tile),
+            device_id_type=pl.DeviceIdType.MESH,
+        ).start()
 
 
 def receipt(source, target, other, capacity, n_tile, send_sem, recv_sem):
@@ -285,7 +292,7 @@
     devices = n_exp * n_tile
     capacity = packed.shape[0] // devices
     me = lax.axis_index("exp") * n_tile + lax.axis_index("tile")
-    greet(me, devices, n_tile)
+    barrier = greet(me, devices, n_tile)
     scale = weight[lax.axis_index("exp"), lax.axis_index("tile")]
 
     def warp(other, target):
@@ -303,14 +310,16 @@
             )
             target[spot] = (scale * second).astype(target.dtype)
 
+    warp(me, arrived)
+    pl.semaphore_wait(barrier, devices - 1)
+
     def step(at, carry):
         other, _ = partner(me, at, devices)
         warp(other, packed)
-        transfer(packed, arrived, me, other, capacity, n_tile, send_sem, recv_sem).start()
+        transfer(packed, arrived, me, other, capacity, n_tile, send_sem, recv_sem)
         return carry
 
     lax.fori_loop(0, devices - 1, step, 0)
-    warp(me, arrived)
 
     hit = route[...] == me
     table[...] = by_rank(hit, ranked(hit), slot[...], SLOT_ROWS * SLOT_COLS, table.shape)
@@ -331,16 +340,19 @@
     capacity = picked.shape[0] // devices
     across = image.shape[1] // BLOCK
     me = lax.axis_index("exp") * n_tile + lax.axis_index("tile")
-    greet(me, devices, n_tile)
+    barrier = greet(me, devices, n_tile)
 
     def pick(other):
         for rank in range(capacity):
             picked[other * capacity + rank] = value[table[other, rank]]
 
+    pick(me)
+    pl.semaphore_wait(barrier, devices - 1)
+
     def begin(at, carry):
         other, _ = partner(me, at, devices)
         pick(other)
-        transfer(picked, returned, me, other, capacity, n_tile, send_sem, recv_sem).start()
+        transfer(picked, returned, me, other, capacity, n_tile, send_sem, recv_sem)
         return carry
 
     lax.fori_loop(0, devices - 1, begin, 0)
@@ -358,7 +370,6 @@
             piece = jnp.dot(back, warp_columns[which], preferred_element_type=jnp.float32)
             unwarped[spot] = piece.astype(unwarped.dtype)
 
-    pick(me)
     unwarp(me, picked)
 
     def finish(at, carry):
@@ -382,7 +393,7 @@
     finish_edges(image, above, below, edge_send, edge_recv)
 
 
-def coadd_kernel(n_tile, table, weight, arrived, patch, value, sums, total):
+def coadd_kernel(n_tile, table, weight, arrived, patch_out, value, sums, total, patch, done):
     slots = SLOT_ROWS * SLOT_COLS
     capacity = arrived.shape[0] // table.shape[0]
     blank = jnp.zeros((BLOCK, BLOCK), jnp.float32)
@@ -414,14 +425,18 @@
                 column * BLOCK : (column + 1) * BLOCK,
             ] = mean
             value[number] = mean.astype(value.dtype)
+        strip = pl.ds(pl.multiple_of(at * BLOCK, BLOCK), BLOCK)
+        pltpu.make_async_copy(patch.at[strip], patch_out.at[strip], done).start()
         return carry
 
     lax.fori_loop(0, SLOT_ROWS, divide, 0)
     value[slots] = blank.astype(value.dtype)
+    pltpu.make_async_copy(patch, patch_out, done).wait()
 
 
 def difference_kernel(
-    coef, above, image, below, row_bands, bands, exposure, difference, padded, passes
+    coef, above, image, below, row_bands, bands, exposure, difference_out, padded, passes,
+    difference, done,
 ):
     cols = image.shape[1]
     row_stage(coef, above, image, below, row_bands, padded, passes)
@@ -431,9 +446,11 @@
         matched = column_chunk(passes, bands, start)
         spot = pl.ds(start, WIDE)
         difference[:, spot] = exposure[:, spot].astype(jnp.float32) - matched
+        pltpu.make_async_copy(difference.at[:, spot], difference_out.at[:, spot], done).start()
         return carry
 
     lax.fori_loop(0, cols // WIDE, step, 0, unroll=2)
+    pltpu.make_async_copy(difference, difference_out, done).wait()
 
 
 def scalars(count):
@@ -442,6 +459,10 @@
 
 def vectors(count):
     return [pl.BlockSpec(memory_space=pltpu.VMEM)] * count
+
+
+def far(count):
+    return [pl.BlockSpec(memory_space=pltpu.HBM)] * count
 
 
 def shards(
@@ -489,9 +510,13 @@
             edge, edge, shape(bases * BLOCK, BLOCK + 2 * RIM), shape(bases, 2 * WIDE, WIDE),
             tables, tables, shape(1, blocks, dtype=jnp.int32),
         ),
-        in_specs=[pl.BlockSpec(memory_space=pl.ANY)] + vectors(4),
+        in_specs=far(1) + vectors(2) + far(2),
         out_specs=tuple(vectors(7)),
-        scratch_shapes=pair,
+        scratch_shapes=pair + [
+            pltpu.VMEM((devices, blocks), jnp.int32),
+            pltpu.VMEM((devices, blocks), jnp.int32),
+            pltpu.SemaphoreType.DMA((2,)),
+        ],
         compiler_params=params(spare + 4, collective_id=2, has_side_effects=True),
     )(mine, row_taps, column_taps, route, warp_id.reshape(devices, blocks))
     matched = pl.pallas_call(
@@ -520,10 +545,12 @@
             shape(slots + 1, BLOCK, BLOCK),
         ),
         in_specs=scalars(2) + vectors(1),
-        out_specs=tuple(vectors(2)),
+        out_specs=tuple(far(1) + vectors(1)),
         scratch_shapes=[
             pltpu.VMEM((slots + 1, BLOCK, BLOCK), jnp.float32),
             pltpu.SMEM((slots + 1,), jnp.float32),
+            pltpu.VMEM((SLOT_ROWS * BLOCK, SLOT_COLS * BLOCK), jnp.float32),
+            pltpu.SemaphoreType.DMA(()),
         ],
         compiler_params=params(buffer_units + 3 * slot_units + spare),
     )(table, weight, arrived)
@@ -542,8 +569,10 @@
         difference_kernel,
         out_shape=shape(rows, cols, dtype=jnp.float32),
         in_specs=scalars(1) + vectors(6),
-        out_specs=pl.BlockSpec(memory_space=pltpu.VMEM),
-        scratch_shapes=work,
+        out_specs=far(1)[0],
+        scratch_shapes=work + [
+            pltpu.VMEM((rows, cols), jnp.float32), pltpu.SemaphoreType.DMA(()),
+        ],
         compiler_params=params(work_units + 4 * image_units + spare),
     )(basis_coef, template_above, template, template_below, row_bands, bands, mine)
     return patch, difference[None]

time: 236 us -> 234 us (level)
  no operation moved by 1% of the time
where the time goes in v5:
time: 234 us
  Pallas kernels  229 us (98%)
  local copies, waits for them, and re-layouts  4.42 us (2%)
    pallas_call x1, Pallas kernels, shards(): pl.pallas_call(functools.partial(return_kernel, n_exp, n_tile), out_shape...  103 us
    pallas_call x1, Pallas kernels, shards(): pl.pallas_call(functools.partial(send_kernel, n_exp, n_tile), out_shape=(...  97.1 us
    pallas_call x1, Pallas kernels, shards(): pl.pallas_call(difference_kernel, out_shape=shape(rows, cols, dtype=jnp.f...  9.3 us
    pallas_call x1, Pallas kernels, shards(): pl.pallas_call(match_kernel, out_shape=shape(blocks + 1, BLOCK, BLOCK), i...  8.29 us
    pallas_call x1, Pallas kernels, shards(): pl.pallas_call(prepare_kernel, out_shape=(edge, edge, shape(bases * BLOCK...  6.73 us

profile of v5, /device:TPU:11, one launch (start us, length us, event | category | flops | bytes accessed | tf_op | source)
XLA Modules:
  0.0 233.9 jit_solution(7698770674346564719)
XLA Ops:
  0.6 0.0 copy-start.9
  0.6 0.0 copy-start
  0.7 1.6 copy-done
  2.2 0.7 copy-done.4
  3.0 0.7 copy-done.6
  3.7 0.7 copy-done.10
  4.4 0.7 copy-done.11
  5.0 6.7 %shard_map.113 = (bf16[16,4096]{1,0:T(8,128)(2,1)S(1)}, bf16[16,4096]{1,0:T(8,128)(2,1)S(1)}, bf16[384,160]{1,0:T(8,128)(2,1)S(1)}, bf16[3,512,256]{2,1,0:T(8,12...) custom-call(bf16[256,4096]{1,0:T(8,128)(2,1)S(1)} %bitcast.5, ...), custom_call_target="tpu_custom_call" | custom-call | tf_op jit(solution)/shard_map/pallas_call | solution.py:507
  11.8 0.0 copy-done.9
  11.8 0.0 copy-done.1
  11.8 0.0 copy-start.2
  11.8 0.0 copy-start.3
  11.8 0.0 copy-start.5
  11.8 0.0 copy-start.7
  11.8 0.0 copy-start.8
  11.8 8.3 %shard_map.114.matched = bf16[65,128,128]{2,1,0:T(8,128)(2,1)S(1)} custom-call(f32[1,3]{1,0:T(1,128)S(1)} %copy-done.9, bf16[16,4096]{1,0:T(8,128)(2,1)S(1)} %get-tuple-element.18.above, bf16[256,4096]{1,0:T(8,128)(2,1)S(1)} %bitcast.6, bf16[16,4096]{1,0:T(8,128)(2,1)S(1)} %get-tuple-element.19.below, bf16[384,160]{1,0:T(8,128)(2,1)S(1)} %get-tuple-element.20.row_bands, ...), custom_call_target="tpu_custom_call" | custom-call | tf_op jit(solution)/shard_map/pallas_call | solution.py:522
  20.2 0.0 copy-done.2
  20.2 0.0 copy-done.3
  20.2 0.0 copy-done.5
  20.2 0.0 copy-done.7
  20.2 97.1 %shard_map.115 = (bf16[128,128,128]{2,1,0:T(8,128)(2,1)S(1)}, s32[32,4]{1,0:T(8,128)S(1)}) custom-call(s32[32,4]{1,0:T(8,128)S(1)} %get-tuple-element.16.source, s32[32,4]{1,0:T(8,128)S(1)} %get-tuple-element.17.ident, f32[4,8]{1,0:T(4,128)S(1)} %copy-done.8, bf16[65,128,128]{2,1,0:T(8,128)(2,1)S(1)} %shard_map.114.matched, ...), custom_call_target="tpu_custom_call" | custom-call | tf_op jit(solution)/shard_map/pallas_call | solution.py:530
  117.3 4.3 %shard_map.116 = (f32[1024,1024]{1,0:T(8,128)}, bf16[65,128,128]{2,1,0:T(8,128)(2,1)S(1)}) custom-call(s32[32,4]{1,0:T(8,128)S(1)} %get-tuple-element.22.table, f32[4,8]{1,0:T(4,128)S(1)} %copy-done.8, bf16[128,128,128]{2,1,0:T(8,128)(2,1)S(1)} %get-tuple-element.23.arrived), custom_call_target="tpu_custom_call" | custom-call | tf_op jit(solution)/shard_map/pallas_call | solution.py:541
  121.7 102.9 %shard_map.117 = (bf16[256,4096]{1,0:T(8,128)(2,1)S(1)}, bf16[16,4096]{1,0:T(8,128)(2,1)S(1)}, bf16[16,4096]{1,0:T(8,128)(2,1)S(1)}) custom-call(s32[32,4]{1,0:T(8,128)S(1)} %get-tuple-element.17.ident, s32[1,64]{1,0:T(1,128)S(1)} %get-tuple-element.25.place, s32[32,4]{1,0:T(8,128)S(1)} %get-tuple-element.22.table, ...), custom_call_target="tpu_custom_call" | custom-call | tf_op jit(solution)/shard_map/pallas_call | solution.py:557
  224.6 9.3 %shard_map.118 = f32[256,4096]{1,0:T(8,128)} custom-call(f32[1,3]{1,0:T(1,128)S(1)} %copy-done.9, bf16[16,4096]{1,0:T(8,128)(2,1)S(1)} %get-tuple-element.27.above, bf16[256,4096]{1,0:T(8,128)(2,1)S(1)} %get-tuple-element.28.image, bf16[16,4096]{1,0:T(8,128)(2,1)S(1)} %get-tuple-element.29.below, bf16[384,160]{1,0:T(8,128)(2,1)S(1)} %get-tuple-element.20.row_bands, ...), custom_call_target="tpu_custom_call" | custom-call | tf_op jit(solution)/shard_map/pallas_call | solution.py:568
  (6 shorter events, 0.0 us)
Async XLA Ops:
  0.6 11.1 %copy-start.9 = (f32[1,3]{1,0:T(1,128)S(1)}, f32[1,3]{1,0:T(1,128)}, u32[]{:S(2)}) copy-start(f32[1,3]{1,0:T(1,128)} %coef.3) | copy-start | bytes 40
  0.6 1.6 copy-start
  2.2 0.7 copy-start.4
  3.0 0.7 copy-start.6
  3.7 0.7 copy-start.10
  4.4 0.7 copy-start.11
  5.0 6.7 %copy-start.1 = (bf16[1,256,4096]{2,1,0:T(8,128)(2,1)S(1)}, bf16[1,256,4096]{2,1,0:T(8,128)(2,1)}, u32[]{:S(2)}) copy-start(bf16[1,256,4096]{2,1,0:T(8,128)(2,1)} %param.10) | copy-start | bytes 6291460
  11.8 8.4 %copy-start.2 = (bf16[64,128,128]{2,1,0:T(8,128)(2,1)S(1)}, bf16[64,128,128]{2,1,0:T(8,128)(2,1)}, u32[]{:S(2)}) copy-start(bf16[64,128,128]{2,1,0:T(8,128)(2,1)} %warp_rows.3) | copy-start | bytes 6291460
  11.8 8.4 %copy-start.3 = (bf16[64,128,128]{2,1,0:T(8,128)(2,1)S(1)}, bf16[64,128,128]{2,1,0:T(8,128)(2,1)}, u32[]{:S(2)}) copy-start(bf16[64,128,128]{2,1,0:T(8,128)(2,1)} %warp_columns.3) | copy-start | bytes 6291460
  11.8 8.4 %copy-start.5 = (s32[4,8,64]{2,1,0:T(8,128)S(1)}, s32[4,8,64]{2,1,0:T(8,128)}, u32[]{:S(2)}) copy-start(s32[4,8,64]{2,1,0:T(8,128)} %param.17) | copy-start | bytes 24580
  11.8 8.4 %copy-start.7 = (s32[4,8,64]{2,1,0:T(8,128)S(1)}, s32[4,8,64]{2,1,0:T(8,128)}, u32[]{:S(2)}) copy-start(s32[4,8,64]{2,1,0:T(8,128)} %param.18) | copy-start | bytes 24580
  11.8 8.4 %copy-start.8 = (f32[4,8]{1,0:T(4,128)S(1)}, f32[4,8]{1,0:T(4,128)}, u32[]{:S(2)}) copy-start(f32[4,8]{1,0:T(4,128)} %weight.3) | copy-start | bytes 388

commit v6 on v5

--- a/solution.py
+++ b/solution.py
@@ -233,15 +233,13 @@
     lax.fori_loop(0, cols // WIDE, step, 0, unroll=2)
 
 
-def partner(me, step, devices):
-    half = devices // 2
-    pair = lax.div(step, 2)
-    odd = lax.rem(pair, 2)
-    far = half + (2 * odd - 1) * lax.div(pair + 1, 2)
-    near = (1 - odd) * (1 + lax.div(pair, 2)) + odd * (devices - 1 - lax.div(pair, 2))
-    turn = lax.rem(step, 2)
-    shift = (1 - turn) * far + turn * near
-    return lax.rem(me + shift, devices), lax.rem(me + devices - shift, devices)
+def partner(me, step, n_exp, n_tile):
+    row, tile = lax.div(me, n_tile), lax.rem(me, n_tile)
+    down = lax.rem(step, n_exp)
+    across = lax.rem(lax.div(step, n_exp) + 2 * down, n_tile)
+    target = lax.rem(row + down, n_exp) * n_tile + lax.rem(tile + across, n_tile)
+    origin = lax.rem(row + n_exp - down, n_exp) * n_tile + lax.rem(tile + n_tile - across, n_tile)
+    return target, origin
 
 
 def address(device, n_tile):
@@ -314,22 +312,22 @@
     pl.semaphore_wait(barrier, devices - 1)
 
     def step(at, carry):
-        other, _ = partner(me, at, devices)
+        other, _ = partner(me, at, n_exp, n_tile)
         warp(other, packed)
         transfer(packed, arrived, me, other, capacity, n_tile, send_sem, recv_sem)
         return carry
 
-    lax.fori_loop(0, devices - 1, step, 0)
+    lax.fori_loop(1, devices, step, 0)
 
     hit = route[...] == me
     table[...] = by_rank(hit, ranked(hit), slot[...], SLOT_ROWS * SLOT_COLS, table.shape)
 
     def finish(at, carry):
-        _, other = partner(me, at, devices)
+        _, other = partner(me, at, n_exp, n_tile)
         receipt(packed, arrived, other, capacity, n_tile, send_sem, recv_sem).wait()
         return carry
 
-    lax.fori_loop(0, devices - 1, finish, 0)
+    lax.fori_loop(1, devices, finish, 0)
 
 
 def return_kernel(
@@ -350,12 +348,12 @@
     pl.semaphore_wait(barrier, devices - 1)
 
     def begin(at, carry):
-        other, _ = partner(me, at, devices)
+        other, _ = partner(me, at, n_exp, n_tile)
         pick(other)
         transfer(picked, returned, me, other, capacity, n_tile, send_sem, recv_sem)
         return carry
 
-    lax.fori_loop(0, devices - 1, begin, 0)
+    lax.fori_loop(1, devices, begin, 0)
 
     def unwarp(other, origin):
         for rank in range(capacity):
@@ -373,12 +371,12 @@
     unwarp(me, picked)
 
     def finish(at, carry):
-        _, other = partner(me, at, devices)
+        _, other = partner(me, at, n_exp, n_tile)
         receipt(picked, returned, other, capacity, n_tile, send_sem, recv_sem).wait()
         unwarp(other, returned)
         return carry
 
-    lax.fori_loop(0, devices - 1, finish, 0)
+    lax.fori_loop(1, devices, finish, 0)
 
     def gather(at, carry):
         left = pl.multiple_of(at * BLOCK, BLOCK)
@@ -517,7 +515,7 @@
             pltpu.VMEM((devices, blocks), jnp.int32),
             pltpu.SemaphoreType.DMA((2,)),
         ],
-        compiler_params=params(spare + 4, collective_id=2, has_side_effects=True),
+        compiler_params=params(56, collective_id=2, has_side_effects=True),
     )(mine, row_taps, column_taps, route, warp_id.reshape(devices, blocks))
     matched = pl.pallas_call(
         match_kernel,

time: 234 us -> 244 us (1.043)
  Pallas kernels: 229 us -> 238 us
    pallas_call x1, Pallas kernels: 103 us -> 110 us  [shards(): pl.pallas_call(functools.partial(return_kernel, n_exp, n_tile), out_shape...]
where the time goes in v6:
time: 244 us; the launch traced here: 243 us
  Pallas kernels  238 us (98%)
  local copies, waits for them, and re-layouts  3.91 us (2%)
    pallas_call x1, Pallas kernels, shards(): pl.pallas_call(functools.partial(return_kernel, n_exp, n_tile), out_shape...  110 us
    pallas_call x1, Pallas kernels, shards(): pl.pallas_call(functools.partial(send_kernel, n_exp, n_tile), out_shape=(...  97.9 us
    pallas_call x1, Pallas kernels, shards(): pl.pallas_call(difference_kernel, out_shape=shape(rows, cols, dtype=jnp.f...  9.31 us
    pallas_call x1, Pallas kernels, shards(): pl.pallas_call(prepare_kernel, out_shape=(edge, edge, shape(bases * BLOCK...  8.84 us
    pallas_call x1, Pallas kernels, shards(): pl.pallas_call(match_kernel, out_shape=shape(blocks + 1, BLOCK, BLOCK), i...  8.29 us

profile of v6, /device:TPU:11, one launch (start us, length us, event | category | flops | bytes accessed | tf_op | source)
XLA Modules:
  0.0 243.1 jit_solution(11997153410100640092)
XLA Ops:
  0.6 0.0 copy-start.14
  0.6 0.0 copy-start
  0.7 8.8 %shard_map.113 = (bf16[16,4096]{1,0:T(8,128)(2,1)}, bf16[16,4096]{1,0:T(8,128)(2,1)}, bf16[384,160]{1,0:T(8,128)(2,1)}, bf16[3,512,256]{2,1,0:T(8,128)(2,1)}, s3...) custom-call(bf16[256,4096]{1,0:T(8,128)(2,1)} %bitcast.5, bf16[3,21]{1,0:T(4,128)(2,1)} %row_taps.1, ...), custom_call_target="tpu_custom_call" | custom-call | tf_op jit(solution)/shard_map/pallas_call | solution.py:505
  9.5 0.0 copy-done.14
  9.5 0.0 copy-done
  9.5 0.0 copy-start.3
  9.5 1.1 copy-done.3
  10.7 0.9 copy-done.5
  11.6 0.9 copy-done.7
  12.5 0.9 copy-done.8
  13.4 0.0 copy-start.11
  13.4 0.0 copy-start.12
  13.4 0.0 copy-start.13
  13.4 8.3 %shard_map.114.matched = bf16[65,128,128]{2,1,0:T(8,128)(2,1)S(1)} custom-call(f32[1,3]{1,0:T(1,128)S(1)} %copy-done.14, bf16[16,4096]{1,0:T(8,128)(2,1)S(1)} %copy-done.7, bf16[256,4096]{1,0:T(8,128)(2,1)S(1)} %bitcast.6, bf16[16,4096]{1,0:T(8,128)(2,1)S(1)} %copy-done.8, bf16[384,160]{1,0:T(8,128)(2,1)S(1)} %copy-done.5, bf16[3,512,256]{2,1,0:T(8,128)(2,1)S(1)} %copy-done.3), custom_call_target="tpu_custom_call" | custom-call | tf_op jit(solution)/shard_map/pallas_call | solution.py:520
  21.7 0.0 copy-done.1
  21.7 0.0 copy-done.2
  21.8 0.0 copy-done.9
  21.8 0.0 copy-done.10
  21.8 0.0 copy-done.11
  21.8 97.9 %shard_map.115 = (bf16[128,128,128]{2,1,0:T(8,128)(2,1)S(1)}, s32[32,4]{1,0:T(8,128)S(1)}) custom-call(s32[32,4]{1,0:T(8,128)S(1)} %copy-done.12, s32[32,4]{1,0:T(8,128)S(1)} %copy-done.10, f32[4,8]{1,0:T(4,128)S(1)} %copy-done.13, bf16[65,128,128]{2,1,0:T(8,128)(2,1)S(1)} %shard_map.114.matched, bf16[64,128,128]{2,1,0:T(8,128)(2,1)S(1)} %copy-done.1, ...), custom_call_target="tpu_custom_call" | custom-call | tf_op jit(solution)/shard_map/pallas_call | solution.py:528
  119.7 0.0 copy-start.15
  119.7 4.3 %shard_map.116 = (f32[1024,1024]{1,0:T(8,128)}, bf16[65,128,128]{2,1,0:T(8,128)(2,1)S(1)}) custom-call(s32[32,4]{1,0:T(8,128)S(1)} %get-tuple-element.22.table, f32[4,8]{1,0:T(4,128)S(1)} %copy-done.13, bf16[128,128,128]{2,1,0:T(8,128)(2,1)S(1)} %get-tuple-element.23.arrived), custom_call_target="tpu_custom_call" | custom-call | tf_op jit(solution)/shard_map/pallas_call | solution.py:539
  124.1 109.6 %shard_map.117 = (bf16[256,4096]{1,0:T(8,128)(2,1)S(1)}, bf16[16,4096]{1,0:T(8,128)(2,1)S(1)}, bf16[16,4096]{1,0:T(8,128)(2,1)S(1)}) custom-call(s32[32,4]{1,0:T(8,128)S(1)} %copy-done.10, s32[1,64]{1,0:T(1,128)S(1)} %copy-done.15, s32[32,4]{1,0:T(8,128)S(1)} %get-tuple-element.22.table, bf16[65,128,128]{2,1,0:T(8,128)(2,1)S(1)} %get-tuple-element.26.value, ...), custom_call_target="tpu_custom_call" | custom-call | tf_op jit(solution)/shard_map/pallas_call | solution.py:555
  233.7 9.3 %shard_map.118 = f32[256,4096]{1,0:T(8,128)} custom-call(f32[1,3]{1,0:T(1,128)S(1)} %copy-done.14, bf16[16,4096]{1,0:T(8,128)(2,1)S(1)} %get-tuple-element.27.above, bf16[256,4096]{1,0:T(8,128)(2,1)S(1)} %get-tuple-element.28.image, bf16[16,4096]{1,0:T(8,128)(2,1)S(1)} %get-tuple-element.29.below, bf16[384,160]{1,0:T(8,128)(2,1)S(1)} %copy-done.6, ...), custom_call_target="tpu_custom_call" | custom-call | tf_op jit(solution)/shard_map/pallas_call | solution.py:566
  (14 shorter events, 0.0 us)
Async XLA Ops:
  0.6 8.9 %copy-start.14 = (f32[1,3]{1,0:T(1,128)S(1)}, f32[1,3]{1,0:T(1,128)}, u32[]{:S(2)}) copy-start(f32[1,3]{1,0:T(1,128)} %coef.3) | copy-start | bytes 40
  0.6 8.9 %copy-start = (bf16[1,256,4096]{2,1,0:T(8,128)(2,1)S(1)}, bf16[1,256,4096]{2,1,0:T(8,128)(2,1)}, u32[]{:S(2)}) copy-start(bf16[1,256,4096]{2,1,0:T(8,128)(2,1)} %param.10) | copy-start | bytes 6291460
  9.5 1.1 copy-start.3
  10.7 0.9 copy-start.5
  11.6 0.9 copy-start.7
  12.5 0.9 copy-start.8
  13.4 8.3 %copy-start.1 = (bf16[64,128,128]{2,1,0:T(8,128)(2,1)S(1)}, bf16[64,128,128]{2,1,0:T(8,128)(2,1)}, u32[]{:S(2)}) copy-start(bf16[64,128,128]{2,1,0:T(8,128)(2,1)} %warp_rows.3) | copy-start | bytes 6291460
  13.4 8.3 %copy-start.2 = (bf16[64,128,128]{2,1,0:T(8,128)(2,1)S(1)}, bf16[64,128,128]{2,1,0:T(8,128)(2,1)}, u32[]{:S(2)}) copy-start(bf16[64,128,128]{2,1,0:T(8,128)(2,1)} %warp_columns.3) | copy-start | bytes 6291460
  13.4 8.4 %copy-start.9 = (s32[4,8,64]{2,1,0:T(8,128)S(1)}, s32[4,8,64]{2,1,0:T(8,128)}, u32[]{:S(2)}) copy-start(s32[4,8,64]{2,1,0:T(8,128)} %param.17) | copy-start | bytes 24580
  13.4 8.4 %copy-start.10 = (s32[32,4]{1,0:T(8,128)S(1)}, s32[32,4]{1,0:T(8,128)}, u32[]{:S(2)}) copy-start(s32[32,4]{1,0:T(8,128)} %get-tuple-element.17.ident) | copy-start | bytes 1540
  13.4 8.4 %copy-start.11 = (s32[4,8,64]{2,1,0:T(8,128)S(1)}, s32[4,8,64]{2,1,0:T(8,128)}, u32[]{:S(2)}) copy-start(s32[4,8,64]{2,1,0:T(8,128)} %param.18) | copy-start | bytes 24580
  13.4 8.4 %copy-start.12 = (s32[32,4]{1,0:T(8,128)S(1)}, s32[32,4]{1,0:T(8,128)}, u32[]{:S(2)}) copy-start(s32[32,4]{1,0:T(8,128)} %get-tuple-element.16.source) | copy-start | bytes 1540
  13.4 8.4 %copy-start.13 = (f32[4,8]{1,0:T(4,128)S(1)}, f32[4,8]{1,0:T(4,128)}, u32[]{:S(2)}) copy-start(f32[4,8]{1,0:T(4,128)} %weight.3) | copy-start | bytes 388
  119.7 4.3 %copy-start.15 = (s32[1,64]{1,0:T(1,128)S(1)}, s32[1,64]{1,0:T(1,128)}, u32[]{:S(2)}) copy-start(s32[1,64]{1,0:T(1,128)} %get-tuple-element.25.place) | copy-start | bytes 772
  124.1 109.6 %copy-start.4 = (bf16[3,512,256]{2,1,0:T(8,128)(2,1)S(1)}, bf16[3,512,256]{2,1,0:T(8,128)(2,1)}, u32[]{:S(2)}) copy-start(bf16[3,512,256]{2,1,0:T(8,128)(2,1)} %get-tuple-element.21.bands) | copy-start | bytes 2359300
  124.1 109.6 %copy-start.6 = (bf16[384,160]{1,0:T(8,128)(2,1)S(1)}, bf16[384,160]{1,0:T(8,128)(2,1)}, u32[]{:S(2)}) copy-start(bf16[384,160]{1,0:T(8,128)(2,1)} %get-tuple-element.20.row_bands) | copy-start | bytes 368644

commit v7 on v6

--- a/solution.py
+++ b/solution.py
@@ -235,8 +235,12 @@
 
 def partner(me, step, n_exp, n_tile):
     row, tile = lax.div(me, n_tile), lax.rem(me, n_tile)
-    down = lax.rem(step, n_exp)
-    across = lax.rem(lax.div(step, n_exp) + 2 * down, n_tile)
+    half = n_exp // 2
+    phase = lax.div(step, 2 * n_tile)
+    side = lax.rem(step, 2)
+    first = jnp.maximum(1 - phase, 0)
+    down = half + phase * (2 * side - 1) - first * (1 - side) * half
+    across = lax.div(lax.rem(step, 2 * n_tile), 2)
     target = lax.rem(row + down, n_exp) * n_tile + lax.rem(tile + across, n_tile)
     origin = lax.rem(row + n_exp - down, n_exp) * n_tile + lax.rem(tile + n_tile - across, n_tile)
     return target, origin
@@ -515,7 +519,7 @@
             pltpu.VMEM((devices, blocks), jnp.int32),
             pltpu.SemaphoreType.DMA((2,)),
         ],
-        compiler_params=params(56, collective_id=2, has_side_effects=True),
+        compiler_params=params(spare + 4, collective_id=2, has_side_effects=True),
     )(mine, row_taps, column_taps, route, warp_id.reshape(devices, blocks))
     matched = pl.pallas_call(
         match_kernel,

time: 244 us -> 238 us (0.975)
  Pallas kernels: 238 us -> 232 us
    pallas_call x1, Pallas kernels: 110 us -> 106 us  [shards(): pl.pallas_call(functools.partial(return_kernel, n_exp, n_tile), out_shape...]
where the time goes in v7:
time: 238 us; the launch traced here: 237 us
  Pallas kernels  232 us (97%)
  local copies, waits for them, and re-layouts  4.42 us (2%)
    pallas_call x1, Pallas kernels, shards(): pl.pallas_call(functools.partial(return_kernel, n_exp, n_tile), out_shape...  106 us
    pallas_call x1, Pallas kernels, shards(): pl.pallas_call(functools.partial(send_kernel, n_exp, n_tile), out_shape=(...  97.8 us
    pallas_call x1, Pallas kernels, shards(): pl.pallas_call(difference_kernel, out_shape=shape(rows, cols, dtype=jnp.f...  9.3 us
    pallas_call x1, Pallas kernels, shards(): pl.pallas_call(match_kernel, out_shape=shape(blocks + 1, BLOCK, BLOCK), i...  8.29 us
    pallas_call x1, Pallas kernels, shards(): pl.pallas_call(prepare_kernel, out_shape=(edge, edge, shape(bases * BLOCK...  6.73 us

profile of v7, /device:TPU:11, one launch (start us, length us, event | category | flops | bytes accessed | tf_op | source)
XLA Modules:
  0.0 237.4 jit_solution(221037595170731704)
XLA Ops:
  0.6 0.0 copy-start.9
  0.6 0.0 copy-start
  0.7 1.6 copy-done
  2.2 0.7 copy-done.4
  3.0 0.7 copy-done.6
  3.7 0.7 copy-done.10
  4.4 0.7 copy-done.11
  5.0 6.7 %shard_map.113 = (bf16[16,4096]{1,0:T(8,128)(2,1)S(1)}, bf16[16,4096]{1,0:T(8,128)(2,1)S(1)}, bf16[384,160]{1,0:T(8,128)(2,1)S(1)}, bf16[3,512,256]{2,1,0:T(8,12...) custom-call(bf16[256,4096]{1,0:T(8,128)(2,1)S(1)} %bitcast.5, ...), custom_call_target="tpu_custom_call" | custom-call | tf_op jit(solution)/shard_map/pallas_call | solution.py:509
  11.8 0.0 copy-done.9
  11.8 0.0 copy-done.1
  11.8 0.0 copy-start.2
  11.8 0.0 copy-start.3
  11.8 0.0 copy-start.5
  11.8 0.0 copy-start.7
  11.8 0.0 copy-start.8
  11.8 8.3 %shard_map.114.matched = bf16[65,128,128]{2,1,0:T(8,128)(2,1)S(1)} custom-call(f32[1,3]{1,0:T(1,128)S(1)} %copy-done.9, bf16[16,4096]{1,0:T(8,128)(2,1)S(1)} %get-tuple-element.18.above, bf16[256,4096]{1,0:T(8,128)(2,1)S(1)} %bitcast.6, bf16[16,4096]{1,0:T(8,128)(2,1)S(1)} %get-tuple-element.19.below, bf16[384,160]{1,0:T(8,128)(2,1)S(1)} %get-tuple-element.20.row_bands, ...), custom_call_target="tpu_custom_call" | custom-call | tf_op jit(solution)/shard_map/pallas_call | solution.py:524
  20.2 0.0 copy-done.2
  20.2 0.0 copy-done.3
  20.2 0.0 copy-done.5
  20.2 0.0 copy-done.7
  20.2 97.8 %shard_map.115 = (bf16[128,128,128]{2,1,0:T(8,128)(2,1)S(1)}, s32[32,4]{1,0:T(8,128)S(1)}) custom-call(s32[32,4]{1,0:T(8,128)S(1)} %get-tuple-element.16.source, s32[32,4]{1,0:T(8,128)S(1)} %get-tuple-element.17.ident, f32[4,8]{1,0:T(4,128)S(1)} %copy-done.8, bf16[65,128,128]{2,1,0:T(8,128)(2,1)S(1)} %shard_map.114.matched, ...), custom_call_target="tpu_custom_call" | custom-call | tf_op jit(solution)/shard_map/pallas_call | solution.py:532
  118.0 4.3 %shard_map.116 = (f32[1024,1024]{1,0:T(8,128)}, bf16[65,128,128]{2,1,0:T(8,128)(2,1)S(1)}) custom-call(s32[32,4]{1,0:T(8,128)S(1)} %get-tuple-element.22.table, f32[4,8]{1,0:T(4,128)S(1)} %copy-done.8, bf16[128,128,128]{2,1,0:T(8,128)(2,1)S(1)} %get-tuple-element.23.arrived), custom_call_target="tpu_custom_call" | custom-call | tf_op jit(solution)/shard_map/pallas_call | solution.py:543
  122.3 105.7 %shard_map.117 = (bf16[256,4096]{1,0:T(8,128)(2,1)S(1)}, bf16[16,4096]{1,0:T(8,128)(2,1)S(1)}, bf16[16,4096]{1,0:T(8,128)(2,1)S(1)}) custom-call(s32[32,4]{1,0:T(8,128)S(1)} %get-tuple-element.17.ident, s32[1,64]{1,0:T(1,128)S(1)} %get-tuple-element.25.place, s32[32,4]{1,0:T(8,128)S(1)} %get-tuple-element.22.table, ...), custom_call_target="tpu_custom_call" | custom-call | tf_op jit(solution)/shard_map/pallas_call | solution.py:559
  228.1 9.3 %shard_map.118 = f32[256,4096]{1,0:T(8,128)} custom-call(f32[1,3]{1,0:T(1,128)S(1)} %copy-done.9, bf16[16,4096]{1,0:T(8,128)(2,1)S(1)} %get-tuple-element.27.above, bf16[256,4096]{1,0:T(8,128)(2,1)S(1)} %get-tuple-element.28.image, bf16[16,4096]{1,0:T(8,128)(2,1)S(1)} %get-tuple-element.29.below, bf16[384,160]{1,0:T(8,128)(2,1)S(1)} %get-tuple-element.20.row_bands, ...), custom_call_target="tpu_custom_call" | custom-call | tf_op jit(solution)/shard_map/pallas_call | solution.py:570
  (6 shorter events, 0.0 us)
Async XLA Ops:
  0.6 11.1 %copy-start.9 = (f32[1,3]{1,0:T(1,128)S(1)}, f32[1,3]{1,0:T(1,128)}, u32[]{:S(2)}) copy-start(f32[1,3]{1,0:T(1,128)} %coef.3) | copy-start | bytes 40
  0.6 1.6 copy-start
  2.2 0.7 copy-start.4
  3.0 0.7 copy-start.6
  3.7 0.7 copy-start.10
  4.4 0.7 copy-start.11
  5.0 6.7 %copy-start.1 = (bf16[1,256,4096]{2,1,0:T(8,128)(2,1)S(1)}, bf16[1,256,4096]{2,1,0:T(8,128)(2,1)}, u32[]{:S(2)}) copy-start(bf16[1,256,4096]{2,1,0:T(8,128)(2,1)} %param.10) | copy-start | bytes 6291460
  11.8 8.4 %copy-start.2 = (bf16[64,128,128]{2,1,0:T(8,128)(2,1)S(1)}, bf16[64,128,128]{2,1,0:T(8,128)(2,1)}, u32[]{:S(2)}) copy-start(bf16[64,128,128]{2,1,0:T(8,128)(2,1)} %warp_rows.3) | copy-start | bytes 6291460
  11.8 8.4 %copy-start.3 = (bf16[64,128,128]{2,1,0:T(8,128)(2,1)S(1)}, bf16[64,128,128]{2,1,0:T(8,128)(2,1)}, u32[]{:S(2)}) copy-start(bf16[64,128,128]{2,1,0:T(8,128)(2,1)} %warp_columns.3) | copy-start | bytes 6291460
  11.8 8.4 %copy-start.5 = (s32[4,8,64]{2,1,0:T(8,128)S(1)}, s32[4,8,64]{2,1,0:T(8,128)}, u32[]{:S(2)}) copy-start(s32[4,8,64]{2,1,0:T(8,128)} %param.17) | copy-start | bytes 24580
  11.8 8.4 %copy-start.7 = (s32[4,8,64]{2,1,0:T(8,128)S(1)}, s32[4,8,64]{2,1,0:T(8,128)}, u32[]{:S(2)}) copy-start(s32[4,8,64]{2,1,0:T(8,128)} %param.18) | copy-start | bytes 24580
  11.8 8.4 %copy-start.8 = (f32[4,8]{1,0:T(4,128)S(1)}, f32[4,8]{1,0:T(4,128)}, u32[]{:S(2)}) copy-start(f32[4,8]{1,0:T(4,128)} %weight.3) | copy-start | bytes 388
